TPU v7x, 1024 devices: a whole 8x8x8 slice. The times are simulated.
1024 devices in a mesh: slab: 64 (over x, y), head: 16 (over z, core).
Axes of the slice: x: 8, y: 8, z: 8, core: 2. Of those that a mesh axis runs over, the one named last changes fastest.
Arguments:
- queries: bfloat16 [131072, 1024], P(('slab', 'head')), may hold values from -8 to 8
- keys: bfloat16 [131072, 1024], P(('slab', 'head')), may hold values from -8 to 8
- values: bfloat16 [131072, 1024], P(('slab', 'head')), may hold values from -6 to 6
- out_grad: bfloat16 [131072, 1024], P(('slab', 'head')), may hold values from -6 to 6
- links: int32 [64, 40, 2], replicated, may hold values from -1 to 79, as said below
- wanted: int32 [64, 64], replicated, may hold values from 0 to 15
Outputs:
- attended: bfloat16 [131072, 1024], P(('slab', 'head'))
- query_grad: bfloat16 [131072, 1024], P(('slab', 'head'))
- key_grad: bfloat16 [131072, 1024], P(('slab', 'head'))
- value_grad: bfloat16 [131072, 1024], P(('slab', 'head'))
Inputs may be any that keep to these rules, and one draw needn't show every extreme that they name: links[t, j] = (query block, key slot). The first 16 links of every slab are (b, b) for b = 0 to 15; the used links come next, then unused ones stored as (-1, 0). Key slot 16 + u never names the slab itself. In every draw some slab uses all 40 links, some slab leaves links unused, and some slab is named by every other slab.
All inputs are finite; a program needn't handle non-finite values.
Results may differ from a plain program's by a relative error of at most 0.011.
Values may be sent and summed in bfloat16 or wider, within the bound.
No kernel may reach another device: no remote copies, remote signals or barrier semaphores. Data moves between devices by JAX's collectives and lax.ppermute only.
A program may use at most 64 MiB of HBM per device.

v0:
```python
import math

import jax
import jax.numpy as jnp
from jax import lax
from jax.sharding import PartitionSpec as P

HD = 64
BLK = 128


highest = lax.Precision.HIGHEST
group_count = 10


def body(queries, keys, values, out_grad, links, wanted):
    slab_count = lax.axis_size("slab")
    slab_index = lax.axis_index("slab")
    q_rows, k_rows, v_rows, g_rows = (
        lax.all_to_all(queries, "head", split_axis=1, concat_axis=0, tiled=True),
        lax.all_to_all(keys, "head", split_axis=1, concat_axis=0, tiled=True),
        lax.all_to_all(values, "head", split_axis=1, concat_axis=0, tiled=True),
        lax.all_to_all(out_grad, "head", split_axis=1, concat_axis=0, tiled=True),
    )
    feature_width = q_rows.shape[1]
    heads_here = feature_width // HD
    blocks = q_rows.shape[0] // BLK
    block_shape = (blocks, BLK, heads_here, HD)
    q_blk = q_rows.reshape(block_shape)
    k_blk = k_rows.reshape(block_shape)
    v_blk = v_rows.reshape(block_shape)
    g_blk = g_rows.reshape(block_shape)
    own_links = lax.dynamic_index_in_dim(links, slab_index, 0, keepdims=False)
    given_blocks = lax.dynamic_index_in_dim(wanted, slab_index, 1, keepdims=False)
    outgoing = jnp.stack([jnp.take(k_blk, given_blocks, 0), jnp.take(v_blk, given_blocks, 0)], 1)
    outgoing = outgoing.reshape(slab_count, 2, BLK * feature_width)
    incoming = lax.all_to_all(outgoing, "slab", split_axis=0, concat_axis=0, tiled=True)
    far_kv = incoming.reshape(slab_count, 2, BLK, heads_here, HD)
    k_table = jnp.concatenate([k_blk, far_kv[:, 0]], 0)
    v_table = jnp.concatenate([v_blk, far_kv[:, 1]], 0)
    score_scale = 1.0 / math.sqrt(HD)
    per_group = own_links.shape[0] // group_count
    link_items = (
        own_links[:, 0].reshape(group_count, per_group),
        own_links[:, 1].reshape(group_count, per_group),
    )
    block_ids = jnp.arange(blocks, dtype=jnp.int32)
    slot_ids = jnp.arange(blocks + slab_count, dtype=jnp.int32)

    def link_scores(queried, key_slot):
        query_safe = jnp.maximum(queried, 0)
        q_sel = jnp.take(q_blk, query_safe, 0)
        k_sel = jnp.take(k_table, key_slot, 0)
        scores = (
            jnp.einsum("gqhd,gkhd->ghqk", q_sel, k_sel, preferred_element_type=jnp.float32)
            * score_scale
        )
        return (query_safe, scores)

    def stat_step(running, link_item):
        row_top, row_total = running
        queried, key_slot = link_item
        query_safe, scores = link_scores(queried, key_slot)
        query_hit = queried[:, None] == block_ids[None, :]
        row_max = scores.max(-1)
        group_top = jnp.max(jnp.where(query_hit[:, :, None, None], row_max[:, None], -1e30), 0)
        new_top = jnp.maximum(row_top, group_top)
        raised = jnp.exp(scores - jnp.take(new_top, query_safe, 0)[..., None])
        row_sums = jnp.where((queried >= 0)[:, None, None], raised.sum(-1), 0.0)
        block_part = jnp.einsum(
            "gn,ghq->nhq", query_hit.astype(jnp.float32), row_sums, precision=highest
        )
        return ((new_top, row_total * jnp.exp(row_top - new_top) + block_part), None)

    start_top = jnp.full((blocks, heads_here, BLK), -1e30, jnp.float32)
    start_total = jnp.zeros((blocks, heads_here, BLK), jnp.float32)
    (row_top, row_total), _ = lax.scan(stat_step, (start_top, start_total), link_items)

    def out_step(running, link_item):
        queried, key_slot = link_item
        query_safe, scores = link_scores(queried, key_slot)
        is_valid = (queried >= 0)[:, None, None, None]
        raised = jnp.exp(scores - jnp.take(row_top, query_safe, 0)[..., None])
        prob_bf = jnp.where(
            is_valid, raised / jnp.take(row_total, query_safe, 0)[..., None], 0.0
        ).astype(jnp.bfloat16)
        v_sel = jnp.take(v_table, key_slot, 0)
        mixed_part = jnp.einsum(
            "ghqk,gkhd->gqhd", prob_bf, v_sel, preferred_element_type=jnp.float32
        )
        query_hit = (queried[:, None] == block_ids[None, :]).astype(jnp.float32)
        block_part = jnp.einsum(
            "gn,gx->nx", query_hit, mixed_part.reshape(per_group, -1), precision=highest
        )
        return (running + block_part, prob_bf)

    out_acc, stored_probs = lax.scan(
        out_step, jnp.zeros((blocks, BLK * feature_width), jnp.float32), link_items
    )
    out_blk = out_acc.reshape(block_shape).astype(jnp.bfloat16)
    out_rows = out_blk.reshape(blocks * BLK, feature_width)
    delta_rows = jnp.transpose(
        jnp.sum(g_blk.astype(jnp.float32) * out_blk.astype(jnp.float32), -1), (0, 2, 1)
    )

    def back_step(running, link_item):
        dq_acc, dkv_acc = running
        queried, key_slot, prob_bf = link_item
        query_safe = jnp.maximum(queried, 0)
        q_sel = jnp.take(q_blk, query_safe, 0)
        k_sel = jnp.take(k_table, key_slot, 0)
        v_sel = jnp.take(v_table, key_slot, 0)
        g_sel = jnp.take(g_blk, query_safe, 0)
        d_prob = jnp.einsum("gqhd,gkhd->ghqk", g_sel, v_sel, preferred_element_type=jnp.float32)
        delta_sel = jnp.take(delta_rows, query_safe, 0)[..., None]
        d_score = (prob_bf.astype(jnp.float32) * (d_prob - delta_sel) * score_scale).astype(
            jnp.bfloat16
        )
        dq_part = jnp.einsum("ghqk,gkhd->gqhd", d_score, k_sel, preferred_element_type=jnp.float32)
        dk_part = jnp.einsum("ghqk,gqhd->gkhd", d_score, q_sel, preferred_element_type=jnp.float32)
        dv_part = jnp.einsum("ghqk,gqhd->gkhd", prob_bf, g_sel, preferred_element_type=jnp.float32)
        query_hit = (queried[:, None] == block_ids[None, :]).astype(jnp.float32)
        slot_hit = ((key_slot[:, None] == slot_ids[None, :]) & (queried >= 0)[:, None]).astype(
            jnp.float32
        )
        dq_acc = dq_acc + jnp.einsum(
            "gn,gx->nx", query_hit, dq_part.reshape(per_group, -1), precision=highest
        )
        both_parts = jnp.stack([dk_part, dv_part], 1).reshape(per_group, -1)
        dkv_acc = dkv_acc + jnp.einsum("gs,gx->sx", slot_hit, both_parts, precision=highest)
        return ((dq_acc, dkv_acc), None)

    start_dq = jnp.zeros((blocks, BLK * feature_width), jnp.float32)
    start_dkv = jnp.zeros((blocks + slab_count, 2 * BLK * feature_width), jnp.float32)
    back_items = (link_items[0], link_items[1], stored_probs)
    (dq_acc, dkv_acc), _ = lax.scan(back_step, (start_dq, start_dkv), back_items)
    far_terms = dkv_acc[blocks:].astype(jnp.bfloat16).reshape(slab_count, 2, BLK * feature_width)
    returned = lax.all_to_all(far_terms, "slab", split_axis=0, concat_axis=0, tiled=True)
    owner_hit = (given_blocks[:, None] == block_ids[None, :]).astype(jnp.float32)
    home_grad = dkv_acc[:blocks] + jnp.einsum(
        "tn,tx->nx",
        owner_hit,
        returned.astype(jnp.float32).reshape(slab_count, -1),
        precision=highest,
    )
    home_grad = home_grad.reshape(blocks, 2, BLK * feature_width).astype(jnp.bfloat16)
    dq_rows = dq_acc.astype(jnp.bfloat16).reshape(blocks * BLK, feature_width)
    dk_rows = home_grad[:, 0].reshape(blocks * BLK, feature_width)
    dv_rows = home_grad[:, 1].reshape(blocks * BLK, feature_width)
    out_back, d_queries, d_keys, d_values = (
        lax.all_to_all(out_rows, "head", split_axis=0, concat_axis=1, tiled=True),
        lax.all_to_all(dq_rows, "head", split_axis=0, concat_axis=1, tiled=True),
        lax.all_to_all(dk_rows, "head", split_axis=0, concat_axis=1, tiled=True),
        lax.all_to_all(dv_rows, "head", split_axis=0, concat_axis=1, tiled=True),
    )
    return (out_back, d_queries, d_keys, d_values)


def solution(mesh):
    in_specs = (
        P(("slab", "head"), None),
        P(("slab", "head"), None),
        P(("slab", "head"), None),
        P(("slab", "head"), None),
        P(),
        P(),
    )
    out_specs = (
        P(("slab", "head"), None),
        P(("slab", "head"), None),
        P(("slab", "head"), None),
        P(("slab", "head"), None),
    )
    return jax.shard_map(body, mesh=mesh, in_specs=in_specs, out_specs=out_specs, check_vma=False)
```

profile of v0, /device:TPU:1, one launch (start us, length us, event | category | flops | bytes accessed | tf_op | source)
XLA Modules:
  0.0 565.3 jit_solution(9628558609919301739)
XLA Ops:
  2.5 18.2 %all-to-all-start = ((bf16[128,16,64]{0,2,1:T(8,128)(2,1)}), bf16[128,16,64]{0,2,1:T(8,128)(2,1)S(1)}, u32[]{:S(2)}, u32[]{:S(2)}) async-start(bf16[128,16,64]{0,2,1:T(8,128)(2,1)} %bitcast.1), calls=%async_computation | async-start | bytes 524288 | tf_op jit(solution)/shard_map/all_to_all | solution.py:22
  24.4 7.9 %all-to-all-done = bf16[128,16,64]{0,2,1:T(8,128)(2,1)S(1)} async-done(((bf16[128,16,64]{0,2,1:T(8,128)(2,1)}), bf16[128,16,64]{0,2,1:T(8,128)(2,1)S(1)}, u32[]{:S(2)}, u32[]{:S(2)}) %all-to-all-start) | async-done | bytes 262176 | tf_op jit(solution)/shard_map/all_to_all | solution.py:22
  36.6 10.3 %all-to-all-done.1 = bf16[128,16,64]{0,2,1:T(8,128)(2,1)S(1)} async-done(((bf16[128,16,64]{0,2,1:T(8,128)(2,1)}), bf16[128,16,64]{0,2,1:T(8,128)(2,1)S(1)}, u32[]{:S(2)}, u32[]{:S(2)}) %all-to-all-start.1) | async-done | bytes 262176 | tf_op jit(solution)/shard_map/all_to_all | solution.py:21
  72.9 13.6 %all-to-all-start.2 = ((bf16[64,2,8192]{2,1,0:T(2,128)(2,1)}), bf16[64,2,8192]{2,1,0:T(2,128)(2,1)}, u32[]{:S(2)}, u32[]{:S(2)}) async-start(bf16[64,2,8192]{2,1,0:T(2,128)(2,1)} %copy.92), calls=%async_computation.2 | async-start | bytes 4194304 | tf_op jit(solution)/shard_map/all_to_all | solution.py:37
  89.2 47.0 %all-to-all-done.2 = bf16[64,2,8192]{2,1,0:T(2,128)(2,1)} async-done(((bf16[64,2,8192]{2,1,0:T(2,128)(2,1)}), bf16[64,2,8192]{2,1,0:T(2,128)(2,1)}, u32[]{:S(2)}, u32[]{:S(2)}) %all-to-all-start.2) | async-done | bytes 2097184 | tf_op jit(solution)/shard_map/all_to_all | solution.py:37
  136.3 9.4 %all-to-all-start.3 = ((bf16[128,16,64]{0,2,1:T(8,128)(2,1)}), bf16[128,16,64]{0,2,1:T(8,128)(2,1)S(1)}, u32[]{:S(2)}, u32[]{:S(2)}) async-start(bf16[128,16,64]{0,2,1:T(8,128)(2,1)} %bitcast.13), calls=%async_computation.3 | async-start | bytes 524288 | tf_op jit(solution)/shard_map/all_to_all | solution.py:20
  149.7 7.0 %reshape.316 = bf16[64,2,128,1,64]{4,2,0,1,3:T(8,128)(2,1)} reshape(bf16[64,2,8192]{2,0,1:T(8,128)(2,1)} %copy.93) | data formatting | bytes 4194304 | tf_op jit(solution)/shard_map/reshape | solution.py:38
  166.1 26.5 %while.39 = (s32[]{:T(128)}, f32[16,1,128]{2,0,1:T(8,128)S(1)}, f32[16,1,128]{2,0,1:T(8,128)S(1)}, s32[10,4]{1,0:T(8,128)S(1)}, bf16[16,128,1,64]{1,3,2,0:T(8,12...) while((s32[]{:T(128)}, f32[16,1,128]{2,0,1:T(8,128)S(1)}, ...), condition=%wide.region_4.9_spmd.clone, body=%wide.region_0.8_spmd.clone.sunk | while | flops 8845483 | bytes 1026544 | solution.py:77
  197.7 64.2 %while.40 = (s32[]{:T(128)}, f32[16,8192]{1,0:T(8,128)S(1)}, bf16[10,4,1,128,128]{4,3,1,2,0:T(8,128)(2,1)}, s32[10,4]{1,0:T(8,128)S(1)}, s32[10,4]{1,0:T(8,128)S...) while((s32[]{:T(128)}, f32[16,8192]{1,0:T(8,128)S(1)}, ...), condition=%wide.region_6.11_spmd.clone, body=%wide.region_5.10_spmd.clone.sunk | while | flops 23759976 | bytes 2847135 | solution.py:97
  264.1 163.5 %while.41 = (s32[]{:T(128)}, f32[16,8192]{1,0:T(8,128)S(1)}, f32[80,16384]{1,0:T(8,128)}, s32[10,4]{1,0:T(8,128)S(1)}, s32[10,4]{1,0:T(8,128)S(1)}, /*index=5*/b...) while((s32[]{:T(128)}, f32[16,8192]{1,0:T(8,128)S(1)}, ...), condition=%wide.region_9.14_spmd.clone, body=%wide.region_8.13_spmd.clone.sunk | while | flops 106204400 | bytes 15944164 | solution.py:136
  287.6 7.2 %convolution_add_fusion.9 = f32[80,16384]{1,0:T(8,128)} fusion(f32[4,16384]{1,0:T(4,128)S(1)} %reshape.631, f32[80,16384]{1,0:T(8,128)} %get-tuple-element.781, pred[]{:T(512)S(6)} %compare.11, s32[4]{0:T(128)S(1)} %get-tuple-element.700, pred[4]{0:T(512)(128)(4,1)S(1)} %get-tuple-element.702), kind=kOutput, calls=%fused_computation.88.clone.1 | convolution fusion | flops 65536640 | bytes 10747925 | tf_op jit(solution)/shard_map/while/body/eval_jaxpr/gs,gx->sx/dot_general | solution.py:130
  304.2 7.2 %convolution_add_fusion.9 = f32[80,16384]{1,0:T(8,128)} fusion(f32[4,16384]{1,0:T(4,128)S(1)} %reshape.631, f32[80,16384]{1,0:T(8,128)} %get-tuple-element.781, pred[]{:T(512)S(6)} %compare.11, s32[4]{0:T(128)S(1)} %get-tuple-element.700, pred[4]{0:T(512)(128)(4,1)S(1)} %get-tuple-element.702), kind=kOutput, calls=%fused_computation.88.clone.1 | convolution fusion | flops 65536640 | bytes 10747925 | tf_op jit(solution)/shard_map/while/body/eval_jaxpr/gs,gx->sx/dot_general | solution.py:130
  320.8 7.2 %convolution_add_fusion.9 = f32[80,16384]{1,0:T(8,128)} fusion(f32[4,16384]{1,0:T(4,128)S(1)} %reshape.631, f32[80,16384]{1,0:T(8,128)} %get-tuple-element.781, pred[]{:T(512)S(6)} %compare.11, s32[4]{0:T(128)S(1)} %get-tuple-element.700, pred[4]{0:T(512)(128)(4,1)S(1)} %get-tuple-element.702), kind=kOutput, calls=%fused_computation.88.clone.1 | convolution fusion | flops 65536640 | bytes 10747925 | tf_op jit(solution)/shard_map/while/body/eval_jaxpr/gs,gx->sx/dot_general | solution.py:130
  337.4 7.2 %convolution_add_fusion.9 = f32[80,16384]{1,0:T(8,128)} fusion(f32[4,16384]{1,0:T(4,128)S(1)} %reshape.631, f32[80,16384]{1,0:T(8,128)} %get-tuple-element.781, pred[]{:T(512)S(6)} %compare.11, s32[4]{0:T(128)S(1)} %get-tuple-element.700, pred[4]{0:T(512)(128)(4,1)S(1)} %get-tuple-element.702), kind=kOutput, calls=%fused_computation.88.clone.1 | convolution fusion | flops 65536640 | bytes 10747925 | tf_op jit(solution)/shard_map/while/body/eval_jaxpr/gs,gx->sx/dot_general | solution.py:130
  354.0 7.2 %convolution_add_fusion.9 = f32[80,16384]{1,0:T(8,128)} fusion(f32[4,16384]{1,0:T(4,128)S(1)} %reshape.631, f32[80,16384]{1,0:T(8,128)} %get-tuple-element.781, pred[]{:T(512)S(6)} %compare.11, s32[4]{0:T(128)S(1)} %get-tuple-element.700, pred[4]{0:T(512)(128)(4,1)S(1)} %get-tuple-element.702), kind=kOutput, calls=%fused_computation.88.clone.1 | convolution fusion | flops 65536640 | bytes 10747925 | tf_op jit(solution)/shard_map/while/body/eval_jaxpr/gs,gx->sx/dot_general | solution.py:130
  370.6 7.2 %convolution_add_fusion.9 = f32[80,16384]{1,0:T(8,128)} fusion(f32[4,16384]{1,0:T(4,128)S(1)} %reshape.631, f32[80,16384]{1,0:T(8,128)} %get-tuple-element.781, pred[]{:T(512)S(6)} %compare.11, s32[4]{0:T(128)S(1)} %get-tuple-element.700, pred[4]{0:T(512)(128)(4,1)S(1)} %get-tuple-element.702), kind=kOutput, calls=%fused_computation.88.clone.1 | convolution fusion | flops 65536640 | bytes 10747925 | tf_op jit(solution)/shard_map/while/body/eval_jaxpr/gs,gx->sx/dot_general | solution.py:130
  387.2 7.2 %convolution_add_fusion.9 = f32[80,16384]{1,0:T(8,128)} fusion(f32[4,16384]{1,0:T(4,128)S(1)} %reshape.631, f32[80,16384]{1,0:T(8,128)} %get-tuple-element.781, pred[]{:T(512)S(6)} %compare.11, s32[4]{0:T(128)S(1)} %get-tuple-element.700, pred[4]{0:T(512)(128)(4,1)S(1)} %get-tuple-element.702), kind=kOutput, calls=%fused_computation.88.clone.1 | convolution fusion | flops 65536640 | bytes 10747925 | tf_op jit(solution)/shard_map/while/body/eval_jaxpr/gs,gx->sx/dot_general | solution.py:130
  403.8 7.2 %convolution_add_fusion.9 = f32[80,16384]{1,0:T(8,128)} fusion(f32[4,16384]{1,0:T(4,128)S(1)} %reshape.631, f32[80,16384]{1,0:T(8,128)} %get-tuple-element.781, pred[]{:T(512)S(6)} %compare.11, s32[4]{0:T(128)S(1)} %get-tuple-element.700, pred[4]{0:T(512)(128)(4,1)S(1)} %get-tuple-element.702), kind=kOutput, calls=%fused_computation.88.clone.1 | convolution fusion | flops 65536640 | bytes 10747925 | tf_op jit(solution)/shard_map/while/body/eval_jaxpr/gs,gx->sx/dot_general | solution.py:130
  420.4 7.2 %convolution_add_fusion.9 = f32[80,16384]{1,0:T(8,128)} fusion(f32[4,16384]{1,0:T(4,128)S(1)} %reshape.631, f32[80,16384]{1,0:T(8,128)} %get-tuple-element.781, pred[]{:T(512)S(6)} %compare.11, s32[4]{0:T(128)S(1)} %get-tuple-element.700, pred[4]{0:T(512)(128)(4,1)S(1)} %get-tuple-element.702), kind=kOutput, calls=%fused_computation.88.clone.1 | convolution fusion | flops 65536640 | bytes 10747925 | tf_op jit(solution)/shard_map/while/body/eval_jaxpr/gs,gx->sx/dot_general | solution.py:130
  435.9 13.4 %all-to-all-start.7 = ((bf16[64,2,8192]{2,1,0:T(2,128)(2,1)}), bf16[64,2,8192]{2,1,0:T(2,128)(2,1)}, u32[]{:S(2)}, u32[]{:S(2)}) async-start(bf16[64,2,8192]{2,1,0:T(2,128)(2,1)} %reshape.319), calls=%async_computation.7 | async-start | bytes 4194304 | tf_op jit(solution)/shard_map/all_to_all | solution.py:138
  450.2 48.4 %all-to-all-done.7 = bf16[64,2,8192]{2,1,0:T(2,128)(2,1)} async-done(((bf16[64,2,8192]{2,1,0:T(2,128)(2,1)}), bf16[64,2,8192]{2,1,0:T(2,128)(2,1)}, u32[]{:S(2)}, u32[]{:S(2)}) %all-to-all-start.7) | async-done | bytes 2097184 | tf_op jit(solution)/shard_map/all_to_all | solution.py:138
  498.6 9.9 %all-to-all-start.4 = ((bf16[16,128,64]{1,2,0:T(8,128)(2,1)}), bf16[16,128,64]{1,2,0:T(8,128)(2,1)S(1)}, u32[]{:S(2)}, u32[]{:S(2)}) async-start(bf16[16,128,64]{1,2,0:T(8,128)(2,1)} %copy.99), calls=%async_computation.4 | async-start | bytes 524288 | tf_op jit(solution)/shard_map/all_to_all | solution.py:151
  539.6 10.2 %all-to-all-done.9 = bf16[16,128,64]{1,2,0:T(8,128)(2,1)S(1)} async-done(((bf16[16,128,64]{1,2,0:T(8,128)(2,1)}), bf16[16,128,64]{1,2,0:T(8,128)(2,1)S(1)}, u32[]{:S(2)}, u32[]{:S(2)}) %all-to-all-start.9) | async-done | bytes 262176 | tf_op jit(solution)/shard_map/all_to_all | solution.py:154
  555.9 8.5 %all-to-all-done.8 = bf16[16,128,64]{1,2,0:T(8,128)(2,1)S(1)} async-done(((bf16[16,128,64]{1,2,0:T(8,128)(2,1)}), bf16[16,128,64]{1,2,0:T(8,128)(2,1)S(1)}, u32[]{:S(2)}, u32[]{:S(2)}) %all-to-all-start.8) | async-done | bytes 262176 | tf_op jit(solution)/shard_map/all_to_all | solution.py:153
  (623 shorter events, 293.4 us)
Async XLA Ops:
  0.6 86.0 %copy-start = (s32[64,40,2]{0,2,1:T(2,128)S(1)}, s32[64,40,2]{0,2,1:T(2,128)}, u32[]{:S(2)}) copy-start(s32[64,40,2]{0,2,1:T(2,128)} %param.24) | copy-start | bytes 61444
  0.6 23.6 %copy-start.7 = (s32[64,64]{1,0:T(8,128)S(1)}, s32[64,64]{1,0:T(8,128)}, u32[]{:S(2)}) copy-start(s32[64,64]{1,0:T(8,128)} %param.25) | copy-start | bytes 49156
  2.5 29.9 %all-to-all-start = ((bf16[128,16,64]{0,2,1:T(8,128)(2,1)}), bf16[128,16,64]{0,2,1:T(8,128)(2,1)S(1)}, u32[]{:S(2)}, u32[]{:S(2)}) async-start(bf16[128,16,64]{0,2,1:T(8,128)(2,1)} %bitcast.1), calls=%async_computation | async-start | bytes 524288 | tf_op jit(solution)/shard_map/all_to_all | solution.py:22
  32.4 14.6 %all-to-all-start.1 = ((bf16[128,16,64]{0,2,1:T(8,128)(2,1)}), bf16[128,16,64]{0,2,1:T(8,128)(2,1)S(1)}, u32[]{:S(2)}, u32[]{:S(2)}) async-start(bf16[128,16,64]{0,2,1:T(8,128)(2,1)} %bitcast.4), calls=%async_computation.1 | async-start | bytes 524288 | tf_op jit(solution)/shard_map/all_to_all | solution.py:21
  46.9 26.0 %all-to-all-start.5 = ((bf16[128,16,64]{0,2,1:T(8,128)(2,1)}), bf16[128,16,64]{0,2,1:T(8,128)(2,1)S(1)}, u32[]{:S(2)}, u32[]{:S(2)}) async-start(bf16[128,16,64]{0,2,1:T(8,128)(2,1)} %bitcast.21), calls=%async_computation.5 | async-start | bytes 524288 | tf_op jit(solution)/shard_map/all_to_all | solution.py:23
  57.6 4.3 copy-start.4
  63.7 4.2 copy-start.5
  72.9 14.1 %copy-start.6 = (bf16[128,1024]{1,0:T(8,128)(2,1)S(1)}, bf16[128,1024]{1,0:T(8,128)(2,1)}, u32[]{:S(2)}) copy-start(bf16[128,1024]{1,0:T(8,128)(2,1)} %param.20) | copy-start | bytes 786436
  72.9 15.2 %copy-start.1 = (bf16[128,16,64]{0,2,1:T(8,128)(2,1)}, bf16[128,16,64]{0,2,1:T(8,128)(2,1)S(1)}, u32[]{:S(2)}) copy-start(bf16[128,16,64]{0,2,1:T(8,128)(2,1)S(1)} %all-to-all-done.5) | copy-start | bytes 786436
  72.9 63.3 %all-to-all-start.2 = ((bf16[64,2,8192]{2,1,0:T(2,128)(2,1)}), bf16[64,2,8192]{2,1,0:T(2,128)(2,1)}, u32[]{:S(2)}, u32[]{:S(2)}) async-start(bf16[64,2,8192]{2,1,0:T(2,128)(2,1)} %copy.92), calls=%async_computation.2 | async-start | bytes 4194304 | tf_op jit(solution)/shard_map/all_to_all | solution.py:37
  136.3 29.8 %all-to-all-start.3 = ((bf16[128,16,64]{0,2,1:T(8,128)(2,1)}), bf16[128,16,64]{0,2,1:T(8,128)(2,1)S(1)}, u32[]{:S(2)}, u32[]{:S(2)}) async-start(bf16[128,16,64]{0,2,1:T(8,128)(2,1)} %bitcast.13), calls=%async_computation.3 | async-start | bytes 524288 | tf_op jit(solution)/shard_map/all_to_all | solution.py:20
  262.5 1.6 copy-start.2
  435.9 13.4 %copy-start.3 = (bf16[16,128,64]{2,1,0:T(8,128)(2,1)S(1)}, bf16[16,128,64]{2,1,0:T(8,128)(2,1)}, u32[]{:S(2)}) copy-start(bf16[16,128,64]{2,1,0:T(8,128)(2,1)} %copy-done.2) | copy-start | bytes 786436
  435.9 62.7 %all-to-all-start.7 = ((bf16[64,2,8192]{2,1,0:T(2,128)(2,1)}), bf16[64,2,8192]{2,1,0:T(2,128)(2,1)}, u32[]{:S(2)}, u32[]{:S(2)}) async-start(bf16[64,2,8192]{2,1,0:T(2,128)(2,1)} %reshape.319), calls=%async_computation.7 | async-start | bytes 4194304 | tf_op jit(solution)/shard_map/all_to_all | solution.py:138
  498.6 21.6 %all-to-all-start.4 = ((bf16[16,128,64]{1,2,0:T(8,128)(2,1)}), bf16[16,128,64]{1,2,0:T(8,128)(2,1)S(1)}, u32[]{:S(2)}, u32[]{:S(2)}) async-start(bf16[16,128,64]{1,2,0:T(8,128)(2,1)} %copy.99), calls=%async_computation.4 | async-start | bytes 524288 | tf_op jit(solution)/shard_map/all_to_all | solution.py:151
  520.2 14.6 %all-to-all-start.6 = ((bf16[16,128,64]{1,2,0:T(8,128)(2,1)}), bf16[16,128,64]{1,2,0:T(8,128)(2,1)S(1)}, u32[]{:S(2)}, u32[]{:S(2)}) async-start(bf16[16,128,64]{1,2,0:T(8,128)(2,1)} %copy.104), calls=%async_computation.6 | async-start | bytes 524288 | tf_op jit(solution)/shard_map/all_to_all | solution.py:152
  534.7 15.1 %all-to-all-start.9 = ((bf16[16,128,64]{1,2,0:T(8,128)(2,1)}), bf16[16,128,64]{1,2,0:T(8,128)(2,1)S(1)}, u32[]{:S(2)}, u32[]{:S(2)}) async-start(bf16[16,128,64]{1,2,0:T(8,128)(2,1)} %copy.108), calls=%async_computation.9 | async-start | bytes 524288 | tf_op jit(solution)/shard_map/all_to_all | solution.py:154
  549.9 14.5 %all-to-all-start.8 = ((bf16[16,128,64]{1,2,0:T(8,128)(2,1)}), bf16[16,128,64]{1,2,0:T(8,128)(2,1)S(1)}, u32[]{:S(2)}, u32[]{:S(2)}) async-start(bf16[16,128,64]{1,2,0:T(8,128)(2,1)} %copy.106), calls=%async_computation.8 | async-start | bytes 524288 | tf_op jit(solution)/shard_map/all_to_all | solution.py:153
where the time goes:
time: 570 us; the launch traced here: 565 us
  local copies, waits for them, and re-layouts  191 us (34%)
  waiting for transfers between devices  143 us (25%)
  matrix products  130 us (23%)
  starting transfers between devices  81.6 us (14%)
  other arithmetic  16.3 us (3%)
    dot_general x10, matrix products, back_step(): jnp.einsum('gs,gx->sx', slot_hit, both_parts, precision=highest)  69.4 us
    all_to_all x1, waiting for transfers between devices, body(): lax.all_to_all(far_terms, 'slab', split_axis=0, concat_axis=0, tiled=True)  48.4 us
    all_to_all x1, waiting for transfers between devices, body(): lax.all_to_all(outgoing, 'slab', split_axis=0, concat_axis=0, tiled=True)  47 us
    gather x10, local copies, waits for them, and re-layouts, out_step(): v_sel = jnp.take(v_table, key_slot, 0)  18.8 us
    gather x10, local copies, waits for them, and re-layouts, back_step(): v_sel = jnp.take(v_table, key_slot, 0)  18.8 us
    all_to_all x1, starting transfers between devices, body(): lax.all_to_all(values, 'head', split_axis=1, concat_axis=0, tiled=True)  18.2 us
    unnamed x26, local copies, waits for them, and re-layouts  17.2 us
    gather x10, local copies, waits for them, and re-layouts, back_step(): g_sel = jnp.take(g_blk, query_safe, 0)  15.1 us
  transfers between devices with their start and end apart: 10, of which 8 were waited for; matrix products, arithmetic and copies ran while one was open for 12% of the time, Pallas kernels for 0%

commit v1 on v0

v1 whole, which is shorter than its diff:
```python
import math

import jax
import jax.numpy as jnp
from jax import lax
from jax.experimental import pallas as pl
from jax.experimental.pallas import tpu as pltpu
from jax.sharding import PartitionSpec as P

HD = 64
BLK = 128
PAIR = 2 * HD
UNROLL = 8
LIMIT = 48 * 1024 * 1024

VMEM = pl.BlockSpec(memory_space=pltpu.VMEM)
SMEM = pl.BlockSpec(memory_space=pltpu.SMEM)


def cost(flops, moved, exps=0):
    return pl.CostEstimate(flops=flops, bytes_accessed=moved, transcendentals=exps)


def pack_kernel(q_ref, k_ref, v_ref, g_ref, out_ref):
    for first_ref, second_ref, row in ((k_ref, v_ref, 0), (q_ref, g_ref, BLK)):
        for h in range(out_ref.shape[0]):
            cols = slice(h * HD, (h + 1) * HD)
            out_ref[h, row : row + BLK, :] = jnp.concatenate(
                [first_ref[:, cols], second_ref[:, cols]], axis=1
            )


def unpack_kernel(in_ref, o_ref, dq_ref, dk_ref, dv_ref):
    for first_ref, second_ref, row in ((dq_ref, o_ref, 0), (dk_ref, dv_ref, BLK)):
        for h in range(0, in_ref.shape[0], 2):
            even = in_ref[h, row : row + BLK, :]
            odd = in_ref[h + 1, row : row + BLK, :]
            cols = slice(h * HD, (h + 2) * HD)
            first_ref[:, cols] = jnp.concatenate([even[:, :HD], odd[:, :HD]], axis=1)
            second_ref[:, cols] = jnp.concatenate([even[:, HD:], odd[:, HD:]], axis=1)


def attend_kernel(
    links_ref,
    near_ref,
    far_ref,
    odq_ref,
    home_ref,
    far_out_ref,
    table,
    masked,
    s_buf,
    d_buf,
    top,
    total,
    delta,
    acc,
    dkv,
):
    blocks, slots = near_ref.shape[0], table.shape[0]
    link_count = links_ref.shape[0]
    score_scale = 1.0 / math.sqrt(HD)
    exp_scale = score_scale * math.log2(math.e)
    left = lax.broadcasted_iota(jnp.int32, (BLK, PAIR), 1) < HD

    for b in range(blocks):
        table[b] = near_ref[b, :BLK, :]
        qg = near_ref[b, BLK:, :]
        masked[b, :BLK, :] = jnp.where(left, qg, jnp.zeros_like(qg))
        masked[b, BLK:, :] = jnp.where(left, jnp.zeros_like(qg), qg)
    table[blocks:] = far_ref[...]
    top[...] = jnp.full_like(top, -3e38)
    total[...] = jnp.zeros_like(total)
    delta[...] = jnp.zeros_like(delta)
    acc[...] = jnp.zeros_like(acc)
    dkv[...] = jnp.zeros_like(dkv)

    def each_link(step):
        def group(i, _):
            for r in range(UNROLL):
                j = i * UNROLL + r
                queried = links_ref[j, 0]
                step(j, jnp.maximum(queried, 0), links_ref[j, 1], queried >= 0)
            return 0

        lax.fori_loop(0, link_count // UNROLL, group, 0)

    def score_step(j, b, s, valid):
        both = lax.dot_general(
            table[s], masked[b], (((1,), (1,)), ((), ())), preferred_element_type=jnp.float32
        )
        s_buf[j] = both[:, :BLK]
        d_buf[j] = both[:, BLK:]
        largest = jnp.max(both[:, :BLK], axis=0, keepdims=True)
        top[b] = jnp.maximum(top[b], jnp.where(valid, largest, -3e38))

    def sum_step(j, b, s, valid):
        shift = top[b] + jnp.where(valid, 0.0, 1e30)
        raised = jnp.exp2((s_buf[j] - shift) * exp_scale)
        s_buf[j] = raised
        total[b] = total[b] + jnp.sum(raised, axis=0, keepdims=True)
        delta[b] = delta[b] + jnp.sum(raised * d_buf[j], axis=0, keepdims=True)

    def grad_step(j, b, s, valid):
        prob = (s_buf[j] * total[b]).astype(jnp.bfloat16)
        dscore = (prob.astype(jnp.float32) * (d_buf[j] - delta[b]) * score_scale).astype(
            jnp.bfloat16
        )
        turned = lax.dot_general(
            table[s],
            jnp.concatenate([prob, dscore], axis=1),
            (((0,), (0,)), ((), ())),
            preferred_element_type=jnp.float32,
        )
        acc[b, :HD, :] += turned[:HD, BLK:]
        acc[b, HD:, :] += turned[HD:, :BLK]
        terms = jnp.dot(
            jnp.concatenate([dscore, prob], axis=0),
            near_ref[b, BLK:, :],
            preferred_element_type=jnp.float32,
        )
        dkv[s] += jnp.where(left, terms[:BLK], terms[BLK:])

    each_link(score_step)
    each_link(sum_step)
    inverse = 1.0 / total[...]
    delta[...] = delta[...] * inverse
    total[...] = inverse
    each_link(grad_step)

    for b in range(blocks):
        odq_ref[b] = acc[b].T.astype(jnp.bfloat16)
    home_ref[...] = dkv[:blocks]
    far_out_ref[...] = dkv[blocks:].astype(jnp.bfloat16)


def combine_kernel(given_ref, home_ref, returned_ref, odq_ref, out_ref, acc):
    acc[...] = home_ref[...]

    def group(i, _):
        for r in range(UNROLL):
            t = i * UNROLL + r
            acc[given_ref[t]] += returned_ref[t].astype(jnp.float32)
        return 0

    lax.fori_loop(0, returned_ref.shape[0] // UNROLL, group, 0)
    out_ref[:, :BLK, :] = odq_ref[...]
    out_ref[:, BLK:, :] = acc[...].astype(jnp.bfloat16)


def body(queries, keys, values, out_grad, links, wanted):
    slabs = lax.axis_size("slab")
    blocks = lax.axis_size("head")
    slab_index = lax.axis_index("slab")
    link_count = links.shape[1]
    slots = blocks + slabs
    bf, f32 = jnp.bfloat16, jnp.float32
    params = pltpu.CompilerParams(vmem_limit_bytes=LIMIT)
    tile = (BLK, PAIR)
    tile_bytes = 2 * BLK * PAIR

    packed = pl.pallas_call(
        pack_kernel,
        out_shape=jax.ShapeDtypeStruct((blocks, 2 * BLK, PAIR), bf),
        in_specs=[VMEM] * 4,
        out_specs=VMEM,
        compiler_params=params,
        cost_estimate=cost(0, 4 * blocks * tile_bytes),
        name="pack",
    )(queries, keys, values, out_grad)
    near = lax.all_to_all(packed, "head", split_axis=0, concat_axis=0, tiled=True)

    own_links = lax.dynamic_index_in_dim(links, slab_index, 0, keepdims=False)
    given = lax.dynamic_index_in_dim(wanted, slab_index, 1, keepdims=False)
    outgoing = jnp.take(near[:, :BLK, :], given, 0)
    far = lax.all_to_all(outgoing, "slab", split_axis=0, concat_axis=0, tiled=True)

    odq, home, far_out = pl.pallas_call(
        attend_kernel,
        out_shape=(
            jax.ShapeDtypeStruct((blocks, *tile), bf),
            jax.ShapeDtypeStruct((blocks, *tile), f32),
            jax.ShapeDtypeStruct((slabs, *tile), bf),
        ),
        in_specs=[SMEM, VMEM, VMEM],
        out_specs=(VMEM, VMEM, VMEM),
        scratch_shapes=[
            pltpu.VMEM((slots, *tile), bf),
            pltpu.VMEM((blocks, 2 * BLK, PAIR), bf),
            pltpu.VMEM((link_count, BLK, BLK), f32),
            pltpu.VMEM((link_count, BLK, BLK), f32),
            pltpu.VMEM((blocks, 1, BLK), f32),
            pltpu.VMEM((blocks, 1, BLK), f32),
            pltpu.VMEM((blocks, 1, BLK), f32),
            pltpu.VMEM((blocks, PAIR, BLK), f32),
            pltpu.VMEM((slots, *tile), f32),
        ],
        compiler_params=params,
        cost_estimate=cost(
            link_count * 6 * BLK * BLK * PAIR * 2,
            (2 * slabs + 4 * blocks) * tile_bytes,
            link_count * BLK * BLK,
        ),
        name="attend",
    )(own_links, near, far)

    returned = lax.all_to_all(far_out, "slab", split_axis=0, concat_axis=0, tiled=True)
    results = pl.pallas_call(
        combine_kernel,
        out_shape=jax.ShapeDtypeStruct((blocks, 2 * BLK, PAIR), bf),
        in_specs=[SMEM, VMEM, VMEM, VMEM],
        out_specs=VMEM,
        scratch_shapes=[pltpu.VMEM((blocks, *tile), f32)],
        compiler_params=params,
        cost_estimate=cost(0, (slabs + 4 * blocks) * tile_bytes),
        name="combine",
    )(given, home, returned, odq)
    mine = lax.all_to_all(results, "head", split_axis=0, concat_axis=0, tiled=True)
    return pl.pallas_call(
        unpack_kernel,
        out_shape=tuple(jax.ShapeDtypeStruct(queries.shape, bf) for _ in range(4)),
        in_specs=[VMEM],
        out_specs=(VMEM,) * 4,
        compiler_params=params,
        cost_estimate=cost(0, 4 * blocks * tile_bytes),
        name="unpack",
    )(mine)


def solution(mesh):
    rows = P(("slab", "head"), None)
    return jax.shard_map(
        body,
        mesh=mesh,
        in_specs=(rows, rows, rows, rows, P(), P()),
        out_specs=(rows,) * 4,
        check_vma=False,
    )
```

time: 570 us -> 239 us (0.42)
  the two profiles are of different devices: /device:TPU:1 before, /device:TPU:127 now
where the time goes in v1:
time: 239 us; the launch traced here: 238 us
  blocking collectives  101 us (42%)
  waiting for transfers between devices  85.2 us (36%)
  starting transfers between devices  28.9 us (12%)
  Pallas kernels  11.1 us (5%)
  local copies, waits for them, and re-layouts  7.61 us (3%)
  other arithmetic  3.54 us (1%)
    all_to_all x1, blocking collectives, body(): lax.all_to_all(far_out, 'slab', split_axis=0, concat_axis=0, tiled=True)  68.5 us
    all_to_all x1, waiting for transfers between devices, body(): lax.all_to_all(outgoing, 'slab', split_axis=0, concat_axis=0, tiled=True)  57.7 us
    all_to_all x1, blocking collectives, body(): lax.all_to_all(results, 'head', split_axis=0, concat_axis=0, tiled=True)  32.8 us
    all_to_all x1, waiting for transfers between devices, body(): lax.all_to_all(packed, 'head', split_axis=0, concat_axis=0, tiled=True)  27.5 us
    all_to_all x1, starting transfers between devices, body(): lax.all_to_all(packed, 'head', split_axis=0, concat_axis=0, tiled=True)  17.4 us
    all_to_all x1, starting transfers between devices, body(): lax.all_to_all(outgoing, 'slab', split_axis=0, concat_axis=0, tiled=True)  11.6 us
    pallas_call x1, Pallas kernels, body(): pl.pallas_call(attend_kernel, out_shape=(jax.ShapeDtypeStruct((blocks, *t...  7.37 us
    unnamed x14, local copies, waits for them, and re-layouts  5.14 us
  transfers between devices with their start and end apart: 2, of which 2 were waited for; matrix products, arithmetic and copies ran while one was open for 0% of the time, Pallas kernels for 0%

profile of v1, /device:TPU:127, one launch (start us, length us, event | category | flops | bytes accessed | tf_op | source)
XLA Modules:
  0.0 238.4 jit_solution(7044508098988286614)
XLA Ops:
  0.6 0.0 copy-start
  0.6 0.0 copy-start.1
  0.7 1.0 copy-done.1
  1.6 0.9 copy-done.2
  2.6 0.9 copy-done.3
  3.5 0.9 copy-done.4
  4.5 1.3 pack.1
  5.8 17.4 %all-to-all-start = ((bf16[16,256,128]{2,1,0:T(8,128)(2,1)}), bf16[16,256,128]{2,1,0:T(8,128)(2,1)S(1)}, u32[]{:S(2)}, u32[]{:S(2)}) async-start(bf16[16,256,128]{2,1,0:T(8,128)(2,1)} %pack.1), calls=%async_computation | async-start | bytes 2097152 | tf_op jit(solution)/shard_map/all_to_all | solution.py:171
  23.1 0.2 fusion
  23.3 0.2 and_reduce_fusion
  23.5 27.5 %all-to-all-done.near_ref = bf16[16,256,128]{2,1,0:T(8,128)(2,1)S(1)} async-done(((bf16[16,256,128]{2,1,0:T(8,128)(2,1)}), bf16[16,256,128]{2,1,0:T(8,128)(2,1)S(1)}, u32[]{:S(2)}, u32[]{:S(2)}) %all-to-all-start) | async-done | bytes 1048608 | tf_op jit(solution)/shard_map/all_to_all | solution.py:171
  51.1 2.1 gather_fusion
  53.3 3.2 %broadcast_select_fusion = bf16[64,128,128]{2,1,0:T(8,128)(2,1)} fusion(bf16[64,128,128]{2,1,0:T(8,128)(2,1)} %gather_fusion, pred[64]{0:T(512)(128)(4,1)S(1)} %and_reduce_fusion), kind=kLoop, calls=%fused_computation.1 | loop fusion | flops 1048576 | bytes 4194368 | tf_op jit(solution)/shard_map/jit(_take)/select_n | solution.py:175
  56.4 11.6 %all-to-all-start.1 = ((bf16[64,128,128]{2,1,0:T(8,128)(2,1)}), bf16[64,128,128]{2,1,0:T(8,128)(2,1)S(1)}, u32[]{:S(2)}, u32[]{:S(2)}) async-start(bf16[64,128,128]{2,1,0:T(8,128)(2,1)} %broadcast_select_fusion), calls=%async_computation.1 | async-start | bytes 4194304 | tf_op jit(solution)/shard_map/all_to_all | solution.py:176
  68.0 0.1 constant_dynamic-slice_fusion
  68.1 0.1 copy.12
  68.2 0.1 copy.13.links_ref
  68.3 57.7 %all-to-all-done.1.far_ref = bf16[64,128,128]{2,1,0:T(8,128)(2,1)S(1)} async-done(((bf16[64,128,128]{2,1,0:T(8,128)(2,1)}), bf16[64,128,128]{2,1,0:T(8,128)(2,1)S(1)}, u32[]{:S(2)}, u32[]{:S(2)}) %all-to-all-start.1) | async-done | bytes 2097184 | tf_op jit(solution)/shard_map/all_to_all | solution.py:176
  126.0 1.3 copy-done.5
  127.3 7.4 %attend.1 = (bf16[16,128,128]{2,1,0:T(8,128)(2,1)S(1)}, f32[16,128,128]{2,1,0:T(8,128)S(1)}, bf16[64,128,128]{2,1,0:T(8,128)(2,1)S(1)}) custom-call(s32[40,2]{1,0:T(8,128)S(1)} %copy.13.links_ref, bf16[16,256,128]{2,1,0:T(8,128)(2,1)S(1)} %all-to-all-done.near_ref, bf16[64,128,128]{2,1,0:T(8,128)(2,1)} %copy-done.5), custom_call_target="tpu_custom_call" | custom-call | flops 1006632960 | bytes 6291456 | tf_op jit(solution)/shard_map/attend/pallas_call | solution.py:178
  134.7 68.5 %all_to_all.20.returned_ref = bf16[64,128,128]{2,1,0:T(8,128)(2,1)S(1)} all-to-all(bf16[64,128,128]{2,1,0:T(8,128)(2,1)S(1)} %get-tuple-element.8), channel_id=1, replica_groups=mesh['slab'=64,'head'=16] {'slab'}, dimensions={0} | all-to-all | bytes 4194304 | tf_op jit(solution)/shard_map/all_to_all | solution.py:207
  203.2 1.2 combine.1
  204.4 32.8 %all_to_all.21.in_ref = bf16[16,256,128]{2,1,0:T(8,128)(2,1)S(1)} all-to-all(bf16[16,256,128]{2,1,0:T(8,128)(2,1)S(1)} %combine.1), channel_id=1, replica_groups=mesh['slab'=64,'head'=16] {'head'}, dimensions={0} | all-to-all | bytes 2097152 | tf_op jit(solution)/shard_map/all_to_all | solution.py:218
  237.1 1.3 unpack.1
  (9 shorter events, 0.1 us)
Async XLA Ops:
  0.6 67.4 %copy-start = (s32[64,40,2]{0,2,1:T(2,128)S(1)}, s32[64,40,2]{0,2,1:T(2,128)}, u32[]{:S(2)}) copy-start(s32[64,40,2]{0,2,1:T(2,128)} %param.10) | copy-start | bytes 61444
  0.6 1.0 copy-start.1
  1.6 0.9 copy-start.2
  2.6 0.9 copy-start.3
  3.5 0.9 copy-start.4
  4.5 18.7 %copy-start.6 = (s32[64,64]{1,0:T(8,128)S(1)}, s32[64,64]{1,0:T(8,128)}, u32[]{:S(2)}) copy-start(s32[64,64]{1,0:T(8,128)} %param.11) | copy-start | bytes 49156
  5.8 45.3 %all-to-all-start = ((bf16[16,256,128]{2,1,0:T(8,128)(2,1)}), bf16[16,256,128]{2,1,0:T(8,128)(2,1)S(1)}, u32[]{:S(2)}, u32[]{:S(2)}) async-start(bf16[16,256,128]{2,1,0:T(8,128)(2,1)} %pack.1), calls=%async_computation | async-start | bytes 2097152 | tf_op jit(solution)/shard_map/all_to_all | solution.py:171
  56.4 69.6 %all-to-all-start.1 = ((bf16[64,128,128]{2,1,0:T(8,128)(2,1)}), bf16[64,128,128]{2,1,0:T(8,128)(2,1)S(1)}, u32[]{:S(2)}, u32[]{:S(2)}) async-start(bf16[64,128,128]{2,1,0:T(8,128)(2,1)} %broadcast_select_fusion), calls=%async_computation.1 | async-start | bytes 4194304 | tf_op jit(solution)/shard_map/all_to_all | solution.py:176
  126.0 1.3 copy-start.5

commit v2 on v1

--- a/solution.py
+++ b/solution.py
@@ -1,3 +1,4 @@
+import functools
 import math
 
 import jax
@@ -38,6 +39,66 @@
             cols = slice(h * HD, (h + 2) * HD)
             first_ref[:, cols] = jnp.concatenate([even[:, :HD], odd[:, :HD]], axis=1)
             second_ref[:, cols] = jnp.concatenate([even[:, HD:], odd[:, HD:]], axis=1)
+
+
+def each_piece(slabs, held):
+    parts = BLK // slabs
+    for c in range(held):
+        for part in range(parts):
+            yield c, slice(part * slabs, (part + 1) * slabs), pl.ds(
+                part * held + c, slabs, stride=parts * held
+            )
+
+
+def spread_kernel(near_ref, out_ref, wide, *, slabs):
+    for c, rows, piece_rows in each_piece(slabs, near_ref.shape[0]):
+        wide[piece_rows, :] = near_ref[c, rows, :].astype(jnp.float32)
+    out_ref[...] = wide[...].astype(jnp.bfloat16)
+
+
+def gather_kernel(hot_ref, in_ref, out_ref, wide, *, slabs, blocks, extra):
+    parts = BLK // slabs
+    pieces = in_ref[...].reshape(slabs, parts, blocks, PAIR)
+    source = jnp.concatenate(
+        [pieces[:, part].reshape(slabs * blocks, PAIR) for part in range(parts)], axis=1
+    )
+    for t in range(0, slabs, UNROLL):
+        picked = jnp.dot(
+            hot_ref[t * extra : (t + UNROLL) * extra, :],
+            source,
+            preferred_element_type=jnp.float32,
+        )
+        for r in range(UNROLL):
+            for part in range(parts):
+                start = ((t + r) * parts + part) * extra
+                wide[start : start + extra, :] = picked[
+                    r * extra : (r + 1) * extra, part * PAIR : (part + 1) * PAIR
+                ]
+    out_ref[...] = wide[...].astype(jnp.bfloat16)
+
+
+def reduce_kernel(hot_ref, in_ref, out_ref, wide, beside, *, slabs, blocks, extra):
+    parts = BLK // slabs
+    wide[...] = in_ref[...].astype(jnp.float32)
+    for t in range(slabs):
+        for part in range(parts):
+            start = (t * parts + part) * extra
+            beside[t * extra : (t + 1) * extra, part * PAIR : (part + 1) * PAIR] = wide[
+                start : start + extra, :
+            ]
+    terms = beside[...].astype(jnp.bfloat16)
+    for u in range(0, slabs, UNROLL):
+        summed = jnp.dot(
+            hot_ref[u * blocks : (u + UNROLL) * blocks, :],
+            terms,
+            preferred_element_type=jnp.float32,
+        ).astype(jnp.bfloat16)
+        for r in range(UNROLL):
+            for part in range(parts):
+                start = ((u + r) * parts + part) * blocks
+                out_ref[start : start + blocks, :] = summed[
+                    r * blocks : (r + 1) * blocks, part * PAIR : (part + 1) * PAIR
+                ]
 
 
 def attend_kernel(
@@ -56,6 +117,9 @@
     delta,
     acc,
     dkv,
+    wide,
+    *,
+    slabs,
 ):
     blocks, slots = near_ref.shape[0], table.shape[0]
     link_count = links_ref.shape[0]
@@ -63,12 +127,14 @@
     exp_scale = score_scale * math.log2(math.e)
     left = lax.broadcasted_iota(jnp.int32, (BLK, PAIR), 1) < HD
 
+    wide[...] = far_ref[...].astype(jnp.float32)
+    for p, rows, piece_rows in each_piece(slabs, slots - blocks):
+        table[blocks + p, rows, :] = wide[piece_rows, :].astype(jnp.bfloat16)
     for b in range(blocks):
         table[b] = near_ref[b, :BLK, :]
         qg = near_ref[b, BLK:, :]
         masked[b, :BLK, :] = jnp.where(left, qg, jnp.zeros_like(qg))
         masked[b, BLK:, :] = jnp.where(left, jnp.zeros_like(qg), qg)
-    table[blocks:] = far_ref[...]
     top[...] = jnp.full_like(top, -3e38)
     total[...] = jnp.zeros_like(total)
     delta[...] = jnp.zeros_like(delta)
@@ -128,24 +194,22 @@
     total[...] = inverse
     each_link(grad_step)
 
+    for p, rows, piece_rows in each_piece(slabs, slots - blocks):
+        wide[piece_rows, :] = dkv[blocks + p, rows, :]
+    far_out_ref[...] = wide[...].astype(jnp.bfloat16)
     for b in range(blocks):
         odq_ref[b] = acc[b].T.astype(jnp.bfloat16)
     home_ref[...] = dkv[:blocks]
-    far_out_ref[...] = dkv[blocks:].astype(jnp.bfloat16)
-
-
-def combine_kernel(given_ref, home_ref, returned_ref, odq_ref, out_ref, acc):
-    acc[...] = home_ref[...]
-
-    def group(i, _):
-        for r in range(UNROLL):
-            t = i * UNROLL + r
-            acc[given_ref[t]] += returned_ref[t].astype(jnp.float32)
-        return 0
-
-    lax.fori_loop(0, returned_ref.shape[0] // UNROLL, group, 0)
+
+
+def combine_kernel(home_ref, returned_ref, odq_ref, out_ref, wide, *, slabs):
+    wide[...] = returned_ref[...].astype(jnp.float32)
+    for c, rows, piece_rows in each_piece(slabs, home_ref.shape[0]):
+        start = BLK + rows.start
+        out_ref[c, start : start + slabs, :] = (
+            home_ref[c, rows, :] + wide[piece_rows, :]
+        ).astype(jnp.bfloat16)
     out_ref[:, :BLK, :] = odq_ref[...]
-    out_ref[:, BLK:, :] = acc[...].astype(jnp.bfloat16)
 
 
 def body(queries, keys, values, out_grad, links, wanted):
@@ -153,11 +217,28 @@
     blocks = lax.axis_size("head")
     slab_index = lax.axis_index("slab")
     link_count = links.shape[1]
-    slots = blocks + slabs
+    extra = link_count - blocks
+    parts = BLK // slabs
     bf, f32 = jnp.bfloat16, jnp.float32
     params = pltpu.CompilerParams(vmem_limit_bytes=LIMIT)
     tile = (BLK, PAIR)
     tile_bytes = 2 * BLK * PAIR
+    sizes = dict(slabs=slabs, blocks=blocks, extra=extra)
+    spread_rows, far_rows = slabs * parts * blocks, slabs * parts * extra
+
+    slots = links[:, blocks:, 1]
+    named = slots - blocks
+    hit = named[:, :, None] == jnp.arange(slabs, dtype=jnp.int32)
+    block_named = jnp.sum(jnp.where(hit, wanted[:, None, :], 0), -1)
+    is_far = (named >= 0) & (links[:, blocks:, 0] >= 0)
+    piece = jnp.where(is_far, named * blocks + block_named, -1).reshape(-1)
+    all_pieces = jnp.arange(slabs * blocks, dtype=jnp.int32)
+    hot = (piece[:, None] == all_pieces[None, :]).astype(bf)
+    hot_turned = (all_pieces[:, None] == piece[None, :]).astype(bf)
+    own_links = lax.dynamic_index_in_dim(links, slab_index, 0, keepdims=False)
+    link_ids = jnp.arange(link_count, dtype=jnp.int32)
+    own_slots = jnp.where(own_links[:, 1] >= blocks, link_ids, own_links[:, 1])
+    own_links = jnp.stack([own_links[:, 0], own_slots], -1)
 
     packed = pl.pallas_call(
         pack_kernel,
@@ -170,22 +251,40 @@
     )(queries, keys, values, out_grad)
     near = lax.all_to_all(packed, "head", split_axis=0, concat_axis=0, tiled=True)
 
-    own_links = lax.dynamic_index_in_dim(links, slab_index, 0, keepdims=False)
-    given = lax.dynamic_index_in_dim(wanted, slab_index, 1, keepdims=False)
-    outgoing = jnp.take(near[:, :BLK, :], given, 0)
-    far = lax.all_to_all(outgoing, "slab", split_axis=0, concat_axis=0, tiled=True)
+    pieces = pl.pallas_call(
+        functools.partial(spread_kernel, slabs=slabs),
+        out_shape=jax.ShapeDtypeStruct((spread_rows, PAIR), bf),
+        in_specs=[VMEM],
+        out_specs=VMEM,
+        scratch_shapes=[pltpu.VMEM((spread_rows, PAIR), f32)],
+        compiler_params=params,
+        cost_estimate=cost(0, 2 * blocks * tile_bytes),
+        name="spread",
+    )(near)
+    pieces = lax.all_to_all(pieces, "slab", split_axis=0, concat_axis=0, tiled=True)
+    chosen = pl.pallas_call(
+        functools.partial(gather_kernel, **sizes),
+        out_shape=jax.ShapeDtypeStruct((far_rows, PAIR), bf),
+        in_specs=[VMEM, VMEM],
+        out_specs=VMEM,
+        scratch_shapes=[pltpu.VMEM((far_rows, PAIR), f32)],
+        compiler_params=params,
+        cost_estimate=cost(2 * far_rows * slabs * blocks * PAIR, 5 * blocks * tile_bytes),
+        name="gather",
+    )(hot, pieces)
+    far = lax.all_to_all(chosen, "slab", split_axis=0, concat_axis=0, tiled=True)
 
     odq, home, far_out = pl.pallas_call(
-        attend_kernel,
+        functools.partial(attend_kernel, slabs=slabs),
         out_shape=(
             jax.ShapeDtypeStruct((blocks, *tile), bf),
             jax.ShapeDtypeStruct((blocks, *tile), f32),
-            jax.ShapeDtypeStruct((slabs, *tile), bf),
+            jax.ShapeDtypeStruct((far_rows, PAIR), bf),
         ),
         in_specs=[SMEM, VMEM, VMEM],
         out_specs=(VMEM, VMEM, VMEM),
         scratch_shapes=[
-            pltpu.VMEM((slots, *tile), bf),
+            pltpu.VMEM((link_count, *tile), bf),
             pltpu.VMEM((blocks, 2 * BLK, PAIR), bf),
             pltpu.VMEM((link_count, BLK, BLK), f32),
             pltpu.VMEM((link_count, BLK, BLK), f32),
@@ -193,28 +292,43 @@
             pltpu.VMEM((blocks, 1, BLK), f32),
             pltpu.VMEM((blocks, 1, BLK), f32),
             pltpu.VMEM((blocks, PAIR, BLK), f32),
-            pltpu.VMEM((slots, *tile), f32),
+            pltpu.VMEM((link_count, *tile), f32),
+            pltpu.VMEM((far_rows, PAIR), f32),
         ],
         compiler_params=params,
         cost_estimate=cost(
             link_count * 6 * BLK * BLK * PAIR * 2,
-            (2 * slabs + 4 * blocks) * tile_bytes,
+            (2 * extra + 4 * blocks) * tile_bytes,
             link_count * BLK * BLK,
         ),
         name="attend",
     )(own_links, near, far)
 
     returned = lax.all_to_all(far_out, "slab", split_axis=0, concat_axis=0, tiled=True)
+    summed = pl.pallas_call(
+        functools.partial(reduce_kernel, **sizes),
+        out_shape=jax.ShapeDtypeStruct((spread_rows, PAIR), bf),
+        in_specs=[VMEM, VMEM],
+        out_specs=VMEM,
+        scratch_shapes=[
+            pltpu.VMEM((far_rows, PAIR), f32),
+            pltpu.VMEM((slabs * extra, parts * PAIR), f32),
+        ],
+        compiler_params=params,
+        cost_estimate=cost(2 * far_rows * slabs * blocks * PAIR, 5 * blocks * tile_bytes),
+        name="reduce",
+    )(hot_turned, returned)
+    summed = lax.all_to_all(summed, "slab", split_axis=0, concat_axis=0, tiled=True)
     results = pl.pallas_call(
-        combine_kernel,
+        functools.partial(combine_kernel, slabs=slabs),
         out_shape=jax.ShapeDtypeStruct((blocks, 2 * BLK, PAIR), bf),
-        in_specs=[SMEM, VMEM, VMEM, VMEM],
-        out_specs=VMEM,
-        scratch_shapes=[pltpu.VMEM((blocks, *tile), f32)],
-        compiler_params=params,
-        cost_estimate=cost(0, (slabs + 4 * blocks) * tile_bytes),
+        in_specs=[VMEM, VMEM, VMEM],
+        out_specs=VMEM,
+        scratch_shapes=[pltpu.VMEM((spread_rows, PAIR), f32)],
+        compiler_params=params,
+        cost_estimate=cost(0, 6 * blocks * tile_bytes),
         name="combine",
-    )(given, home, returned, odq)
+    )(home, summed, odq)
     mine = lax.all_to_all(results, "head", split_axis=0, concat_axis=0, tiled=True)
     return pl.pallas_call(
         unpack_kernel,

time: 239 us -> 223 us (0.933)
  the two profiles are of different devices: /device:TPU:127 before, /device:TPU:1 now
where the time goes in v2:
time: 223 us; the launch traced here: 222 us
  waiting for transfers between devices  83.9 us (38%)
  blocking collectives  61.1 us (27%)
  starting transfers between devices  46.5 us (21%)
  Pallas kernels  17.8 us (8%)
  local copies, waits for them, and re-layouts  8.54 us (4%)
  other arithmetic  3.29 us (1%)
    all_to_all x1, blocking collectives, body(): lax.all_to_all(results, 'head', split_axis=0, concat_axis=0, tiled=True)  35.5 us
    all_to_all x1, waiting for transfers between devices, body(): lax.all_to_all(packed, 'head', split_axis=0, concat_axis=0, tiled=True)  27.8 us
    all_to_all x1, blocking collectives, body(): lax.all_to_all(summed, 'slab', split_axis=0, concat_axis=0, tiled=True)  25.6 us
    all_to_all x1, waiting for transfers between devices, body(): lax.all_to_all(chosen, 'slab', split_axis=0, concat_axis=0, tiled=True)  21.3 us
    all_to_all x1, waiting for transfers between devices, body(): lax.all_to_all(far_out, 'slab', split_axis=0, concat_axis=0, tiled=True)  19.4 us
    all_to_all x1, starting transfers between devices, body(): lax.all_to_all(packed, 'head', split_axis=0, concat_axis=0, tiled=True)  18.2 us
    all_to_all x1, waiting for transfers between devices, body(): lax.all_to_all(pieces, 'slab', split_axis=0, concat_axis=0, tiled=True)  15.4 us
    all_to_all x1, starting transfers between devices, body(): lax.all_to_all(pieces, 'slab', split_axis=0, concat_axis=0, tiled=True)  13.5 us
  transfers between devices with their start and end apart: 4, of which 4 were waited for; matrix products, arithmetic and copies ran while one was open for 2% of the time, Pallas kernels for 0%

profile of v2, /device:TPU:1, one launch (start us, length us, event | category | flops | bytes accessed | tf_op | source)
XLA Modules:
  0.0 222.0 jit_solution(17246497543784218961)
XLA Ops:
  0.6 0.9 copy-done.7
  1.6 0.9 copy-done.8
  2.5 0.9 copy-done.9
  3.5 0.9 copy-done.10
  4.4 1.3 pack.1
  5.8 18.2 %all-to-all-start = ((bf16[16,256,128]{2,1,0:T(8,128)(2,1)}), bf16[16,256,128]{2,1,0:T(8,128)(2,1)S(1)}, u32[]{:S(2)}, u32[]{:S(2)}) async-start(bf16[16,256,128]{2,1,0:T(8,128)(2,1)} %pack.1), calls=%async_computation | async-start | bytes 2097152 | tf_op jit(solution)/shard_map/all_to_all | solution.py:252
  24.1 27.8 %all-to-all-done.near_ref = bf16[16,256,128]{2,1,0:T(8,128)(2,1)S(1)} async-done(((bf16[16,256,128]{2,1,0:T(8,128)(2,1)}), bf16[16,256,128]{2,1,0:T(8,128)(2,1)S(1)}, u32[]{:S(2)}, u32[]{:S(2)}) %all-to-all-start) | async-done | bytes 1048608 | tf_op jit(solution)/shard_map/all_to_all | solution.py:252
  51.9 1.9 spread.1
  53.8 13.5 %all-to-all-start.1 = ((bf16[64,32,128]{2,1,0:T(8,128)(2,1)}), bf16[64,32,128]{2,1,0:T(8,128)(2,1)}, u32[]{:S(2)}, u32[]{:S(2)}) async-start(bf16[64,32,128]{2,1,0:T(8,128)(2,1)} %bitcast.2), calls=%async_computation.1 | async-start | bytes 1048576 | tf_op jit(solution)/shard_map/all_to_all | solution.py:264
  67.3 1.4 select_reduce_fusion
  69.8 15.4 %all-to-all-done.1 = bf16[64,32,128]{2,1,0:T(8,128)(2,1)} async-done(((bf16[64,32,128]{2,1,0:T(8,128)(2,1)}), bf16[64,32,128]{2,1,0:T(8,128)(2,1)}, u32[]{:S(2)}, u32[]{:S(2)}) %all-to-all-start.1) | async-done | bytes 524320 | tf_op jit(solution)/shard_map/all_to_all | solution.py:264
  85.2 2.0 gather.1
  88.2 6.1 %all-to-all-start.2 = ((bf16[64,48,128]{2,1,0:T(8,128)(2,1)}), bf16[64,48,128]{2,1,0:T(8,128)(2,1)S(1)}, u32[]{:S(2)}, u32[]{:S(2)}) async-start(bf16[64,48,128]{2,1,0:T(8,128)(2,1)} %bitcast.14), calls=%async_computation.2 | async-start | bytes 1572864 | tf_op jit(solution)/shard_map/all_to_all | solution.py:275
  94.6 21.3 %all-to-all-done.2 = bf16[64,48,128]{2,1,0:T(8,128)(2,1)S(1)} async-done(((bf16[64,48,128]{2,1,0:T(8,128)(2,1)}), bf16[64,48,128]{2,1,0:T(8,128)(2,1)S(1)}, u32[]{:S(2)}, u32[]{:S(2)}) %all-to-all-start.2) | async-done | bytes 786464 | tf_op jit(solution)/shard_map/all_to_all | solution.py:275
  115.9 1.2 copy-done.1
  117.1 8.4 %attend.1 = (bf16[16,128,128]{2,1,0:T(8,128)(2,1)S(1)}, f32[16,128,128]{2,1,0:T(8,128)S(1)}, bf16[3072,128]{1,0:T(8,128)(2,1)}) custom-call(s32[40,2]{1,0:T(8,128)S(1)} %copy.29.links_ref, bf16[16,256,128]{2,1,0:T(8,128)(2,1)S(1)} %copy-done.1, bf16[3072,128]{1,0:T(8,128)(2,1)S(1)} %bitcast.17), custom_call_target="tpu_custom_call" | custom-call | flops 1006632960 | bytes 3670016 | tf_op jit(solution)/shard_map/attend/pallas_call | solution.py:277
  125.5 1.0 copy-done.3
  127.3 8.7 %all-to-all-start.3 = ((bf16[64,48,128]{2,1,0:T(8,128)(2,1)}), bf16[64,48,128]{2,1,0:T(8,128)(2,1)}, u32[]{:S(2)}, u32[]{:S(2)}) async-start(bf16[64,48,128]{2,1,0:T(8,128)(2,1)} %bitcast.6), calls=%async_computation.3 | async-start | bytes 1572864 | tf_op jit(solution)/shard_map/all_to_all | solution.py:307
  136.0 1.3 fusion.1.hot_ref
  137.3 19.4 %all-to-all-done.3 = bf16[64,48,128]{2,1,0:T(8,128)(2,1)} async-done(((bf16[64,48,128]{2,1,0:T(8,128)(2,1)}), bf16[64,48,128]{2,1,0:T(8,128)(2,1)}, u32[]{:S(2)}, u32[]{:S(2)}) %all-to-all-start.3) | async-done | bytes 786464 | tf_op jit(solution)/shard_map/all_to_all | solution.py:307
  156.6 2.2 %reduce.1 = bf16[2048,128]{1,0:T(8,128)(2,1)S(1)} custom-call(bf16[1024,1536]{1,0:T(8,128)(2,1)S(1)} %fusion.1.hot_ref, bf16[3072,128]{1,0:T(8,128)(2,1)} %bitcast.7.in_ref), custom_call_target="tpu_custom_call" | custom-call | flops 805306368 | bytes 2621440 | tf_op jit(solution)/shard_map/reduce/pallas_call | solution.py:308
  158.9 25.6 %all_to_all.54 = bf16[64,32,128]{2,1,0:T(8,128)(2,1)S(1)} all-to-all(bf16[64,32,128]{2,1,0:T(8,128)(2,1)S(1)} %bitcast.15), channel_id=1, replica_groups=mesh['slab'=64,'head'=16] {'slab'}, dimensions={0} | all-to-all | bytes 1048576 | tf_op jit(solution)/shard_map/all_to_all | solution.py:321
  185.2 35.5 %all_to_all.55.in_ref = bf16[16,256,128]{2,1,0:T(8,128)(2,1)S(1)} all-to-all(bf16[16,256,128]{2,1,0:T(8,128)(2,1)S(1)} %combine.1), channel_id=1, replica_groups=mesh['slab'=64,'head'=16] {'head'}, dimensions={0} | all-to-all | bytes 2097152 | tf_op jit(solution)/shard_map/all_to_all | solution.py:332
  220.7 1.3 unpack.1
  (36 shorter events, 3.9 us)
Async XLA Ops:
  0.6 1.0 copy-start.7
  1.6 0.9 copy-start.8
  2.5 0.9 copy-start.9
  3.5 0.9 copy-start.10
  4.4 19.5 %copy-start.11 = (s32[64,40,2]{0,2,1:T(2,128)S(1)}, s32[64,40,2]{0,2,1:T(2,128)}, u32[]{:S(2)}) copy-start(s32[64,40,2]{0,2,1:T(2,128)} %param.10) | copy-start | bytes 61444
  4.4 62.9 %copy-start.12 = (s32[64,64]{1,0:T(8,128)S(1)}, s32[64,64]{1,0:T(8,128)}, u32[]{:S(2)}) copy-start(s32[64,64]{1,0:T(8,128)} %param.11) | copy-start | bytes 49156
  5.8 46.1 %all-to-all-start = ((bf16[16,256,128]{2,1,0:T(8,128)(2,1)}), bf16[16,256,128]{2,1,0:T(8,128)(2,1)S(1)}, u32[]{:S(2)}, u32[]{:S(2)}) async-start(bf16[16,256,128]{2,1,0:T(8,128)(2,1)} %pack.1), calls=%async_computation | async-start | bytes 2097152 | tf_op jit(solution)/shard_map/all_to_all | solution.py:252
  51.9 17.3 %copy-start = (bf16[16,256,128]{2,1,0:T(8,128)(2,1)}, bf16[16,256,128]{2,1,0:T(8,128)(2,1)S(1)}, u32[]{:S(2)}) copy-start(bf16[16,256,128]{2,1,0:T(8,128)(2,1)S(1)} %all-to-all-done.near_ref) | copy-start | bytes 3145732
  53.8 31.4 %all-to-all-start.1 = ((bf16[64,32,128]{2,1,0:T(8,128)(2,1)}), bf16[64,32,128]{2,1,0:T(8,128)(2,1)}, u32[]{:S(2)}, u32[]{:S(2)}) async-start(bf16[64,32,128]{2,1,0:T(8,128)(2,1)} %bitcast.2), calls=%async_computation.1 | async-start | bytes 1048576 | tf_op jit(solution)/shard_map/all_to_all | solution.py:264
  87.2 0.9 copy-start.2
  88.2 27.8 %all-to-all-start.2 = ((bf16[64,48,128]{2,1,0:T(8,128)(2,1)}), bf16[64,48,128]{2,1,0:T(8,128)(2,1)S(1)}, u32[]{:S(2)}, u32[]{:S(2)}) async-start(bf16[64,48,128]{2,1,0:T(8,128)(2,1)} %bitcast.14), calls=%async_computation.2 | async-start | bytes 1572864 | tf_op jit(solution)/shard_map/all_to_all | solution.py:275
  115.9 1.2 copy-start.1
  125.5 1.0 copy-start.3
  126.5 0.8 copy-start.5
  127.3 29.4 %all-to-all-start.3 = ((bf16[64,48,128]{2,1,0:T(8,128)(2,1)}), bf16[64,48,128]{2,1,0:T(8,128)(2,1)}, u32[]{:S(2)}, u32[]{:S(2)}) async-start(bf16[64,48,128]{2,1,0:T(8,128)(2,1)} %bitcast.6), calls=%async_computation.3 | async-start | bytes 1572864 | tf_op jit(solution)/shard_map/all_to_all | solution.py:307
  156.6 27.8 %copy-start.4 = (f32[16,128,128]{2,1,0:T(8,128)S(1)}, f32[16,128,128]{2,1,0:T(8,128)}, u32[]{:S(2)}) copy-start(f32[16,128,128]{2,1,0:T(8,128)} %copy-done.3) | copy-start | bytes 3145732
  156.6 27.8 %copy-start.6 = (bf16[16,128,128]{2,1,0:T(8,128)(2,1)S(1)}, bf16[16,128,128]{2,1,0:T(8,128)(2,1)}, u32[]{:S(2)}) copy-start(bf16[16,128,128]{2,1,0:T(8,128)(2,1)} %copy-done.5) | copy-start | bytes 1572868

commit v3 on v2

--- a/solution.py
+++ b/solution.py
@@ -16,26 +16,45 @@
 
 VMEM = pl.BlockSpec(memory_space=pltpu.VMEM)
 SMEM = pl.BlockSpec(memory_space=pltpu.SMEM)
+ANY = pl.BlockSpec(memory_space=pl.ANY)
 
 
 def cost(flops, moved, exps=0):
     return pl.CostEstimate(flops=flops, bytes_accessed=moved, transcendentals=exps)
 
 
-def pack_kernel(q_ref, k_ref, v_ref, g_ref, out_ref):
-    for first_ref, second_ref, row in ((k_ref, v_ref, 0), (q_ref, g_ref, BLK)):
+def pack_kernel(k_ref, v_ref, q_ref, g_ref, kv_ref, qg_ref, held, sems):
+    copies = [
+        pltpu.make_async_copy(ref, held.at[i], sems.at[i])
+        for i, ref in enumerate((k_ref, v_ref, q_ref, g_ref))
+    ]
+    for copy in copies:
+        copy.start()
+    for first, out_ref in ((0, kv_ref), (2, qg_ref)):
+        copies[first].wait()
+        copies[first + 1].wait()
         for h in range(out_ref.shape[0]):
             cols = slice(h * HD, (h + 1) * HD)
-            out_ref[h, row : row + BLK, :] = jnp.concatenate(
-                [first_ref[:, cols], second_ref[:, cols]], axis=1
-            )
-
-
-def unpack_kernel(in_ref, o_ref, dq_ref, dk_ref, dv_ref):
-    for first_ref, second_ref, row in ((dq_ref, o_ref, 0), (dk_ref, dv_ref, BLK)):
-        for h in range(0, in_ref.shape[0], 2):
-            even = in_ref[h, row : row + BLK, :]
-            odd = in_ref[h + 1, row : row + BLK, :]
+            out_ref[h] = jnp.concatenate([held[first, :, cols], held[first + 1, :, cols]], axis=1)
+
+
+def own_tiles(all_ref, index, held, sems):
+    return [
+        pltpu.make_async_copy(all_ref.at[i, index], held.at[i], sems.at[i])
+        for i in range(held.shape[0])
+    ]
+
+
+def unpack_kernel(index_ref, odq_ref, dkv_ref, o_ref, dq_ref, dk_ref, dv_ref, held, sems):
+    copies = own_tiles(odq_ref, index_ref[0], held, sems)
+    for copy in copies:
+        copy.start()
+    for tiles, first_ref, second_ref in ((dkv_ref, dk_ref, dv_ref), (held, dq_ref, o_ref)):
+        if tiles is held:
+            for copy in copies:
+                copy.wait()
+        for h in range(0, tiles.shape[0], 2):
+            even, odd = tiles[h], tiles[h + 1]
             cols = slice(h * HD, (h + 2) * HD)
             first_ref[:, cols] = jnp.concatenate([even[:, :HD], odd[:, :HD]], axis=1)
             second_ref[:, cols] = jnp.concatenate([even[:, HD:], odd[:, HD:]], axis=1)
@@ -102,9 +121,11 @@
 
 
 def attend_kernel(
+    index_ref,
     links_ref,
     near_ref,
     far_ref,
+    all_qg_ref,
     odq_ref,
     home_ref,
     far_out_ref,
@@ -118,9 +139,14 @@
     acc,
     dkv,
     wide,
+    qg,
+    sems,
     *,
     slabs,
 ):
+    copies = own_tiles(all_qg_ref, index_ref[0], qg, sems)
+    for copy in copies:
+        copy.start()
     blocks, slots = near_ref.shape[0], table.shape[0]
     link_count = links_ref.shape[0]
     score_scale = 1.0 / math.sqrt(HD)
@@ -131,15 +157,18 @@
     for p, rows, piece_rows in each_piece(slabs, slots - blocks):
         table[blocks + p, rows, :] = wide[piece_rows, :].astype(jnp.bfloat16)
     for b in range(blocks):
-        table[b] = near_ref[b, :BLK, :]
-        qg = near_ref[b, BLK:, :]
-        masked[b, :BLK, :] = jnp.where(left, qg, jnp.zeros_like(qg))
-        masked[b, BLK:, :] = jnp.where(left, jnp.zeros_like(qg), qg)
+        table[b] = near_ref[b]
     top[...] = jnp.full_like(top, -3e38)
     total[...] = jnp.zeros_like(total)
     delta[...] = jnp.zeros_like(delta)
     acc[...] = jnp.zeros_like(acc)
     dkv[...] = jnp.zeros_like(dkv)
+    for copy in copies:
+        copy.wait()
+    for b in range(blocks):
+        own = qg[b]
+        masked[b, :BLK, :] = jnp.where(left, own, jnp.zeros_like(own))
+        masked[b, BLK:, :] = jnp.where(left, jnp.zeros_like(own), own)
 
     def each_link(step):
         def group(i, _):
@@ -182,7 +211,7 @@
         acc[b, HD:, :] += turned[HD:, :BLK]
         terms = jnp.dot(
             jnp.concatenate([dscore, prob], axis=0),
-            near_ref[b, BLK:, :],
+            qg[b],
             preferred_element_type=jnp.float32,
         )
         dkv[s] += jnp.where(left, terms[:BLK], terms[BLK:])
@@ -202,14 +231,10 @@
     home_ref[...] = dkv[:blocks]
 
 
-def combine_kernel(home_ref, returned_ref, odq_ref, out_ref, wide, *, slabs):
+def combine_kernel(home_ref, returned_ref, out_ref, wide, *, slabs):
     wide[...] = returned_ref[...].astype(jnp.float32)
     for c, rows, piece_rows in each_piece(slabs, home_ref.shape[0]):
-        start = BLK + rows.start
-        out_ref[c, start : start + slabs, :] = (
-            home_ref[c, rows, :] + wide[piece_rows, :]
-        ).astype(jnp.bfloat16)
-    out_ref[:, :BLK, :] = odq_ref[...]
+        out_ref[c, rows, :] = (home_ref[c, rows, :] + wide[piece_rows, :]).astype(jnp.bfloat16)
 
 
 def body(queries, keys, values, out_grad, links, wanted):
@@ -240,16 +265,21 @@
     own_slots = jnp.where(own_links[:, 1] >= blocks, link_ids, own_links[:, 1])
     own_links = jnp.stack([own_links[:, 0], own_slots], -1)
 
-    packed = pl.pallas_call(
+    own_index = lax.axis_index("head").astype(jnp.int32).reshape(1)
+    kv, qg = pl.pallas_call(
         pack_kernel,
-        out_shape=jax.ShapeDtypeStruct((blocks, 2 * BLK, PAIR), bf),
-        in_specs=[VMEM] * 4,
-        out_specs=VMEM,
-        compiler_params=params,
+        out_shape=(jax.ShapeDtypeStruct((blocks, *tile), bf),) * 2,
+        in_specs=[ANY] * 4,
+        out_specs=(VMEM,) * 2,
+        scratch_shapes=[
+            pltpu.VMEM((4, *queries.shape), bf),
+            pltpu.SemaphoreType.DMA((4,)),
+        ],
         cost_estimate=cost(0, 4 * blocks * tile_bytes),
         name="pack",
-    )(queries, keys, values, out_grad)
-    near = lax.all_to_all(packed, "head", split_axis=0, concat_axis=0, tiled=True)
+    )(keys, values, queries, out_grad)
+    near = lax.all_to_all(kv, "head", split_axis=0, concat_axis=0, tiled=True)
+    all_qg = lax.all_gather(qg, "head")
 
     pieces = pl.pallas_call(
         functools.partial(spread_kernel, slabs=slabs),
@@ -281,7 +311,7 @@
             jax.ShapeDtypeStruct((blocks, *tile), f32),
             jax.ShapeDtypeStruct((far_rows, PAIR), bf),
         ),
-        in_specs=[SMEM, VMEM, VMEM],
+        in_specs=[SMEM, SMEM, VMEM, VMEM, ANY],
         out_specs=(VMEM, VMEM, VMEM),
         scratch_shapes=[
             pltpu.VMEM((link_count, *tile), bf),
@@ -294,6 +324,8 @@
             pltpu.VMEM((blocks, PAIR, BLK), f32),
             pltpu.VMEM((link_count, *tile), f32),
             pltpu.VMEM((far_rows, PAIR), f32),
+            pltpu.VMEM((blocks, *tile), bf),
+            pltpu.SemaphoreType.DMA((blocks,)),
         ],
         compiler_params=params,
         cost_estimate=cost(
@@ -302,7 +334,8 @@
             link_count * BLK * BLK,
         ),
         name="attend",
-    )(own_links, near, far)
+    )(own_index, own_links, near, far, all_qg)
+    all_odq = lax.all_gather(odq, "head")
 
     returned = lax.all_to_all(far_out, "slab", split_axis=0, concat_axis=0, tiled=True)
     summed = pl.pallas_call(
@@ -319,26 +352,29 @@
         name="reduce",
     )(hot_turned, returned)
     summed = lax.all_to_all(summed, "slab", split_axis=0, concat_axis=0, tiled=True)
-    results = pl.pallas_call(
+    dkv = pl.pallas_call(
         functools.partial(combine_kernel, slabs=slabs),
-        out_shape=jax.ShapeDtypeStruct((blocks, 2 * BLK, PAIR), bf),
-        in_specs=[VMEM, VMEM, VMEM],
+        out_shape=jax.ShapeDtypeStruct((blocks, *tile), bf),
+        in_specs=[VMEM, VMEM],
         out_specs=VMEM,
         scratch_shapes=[pltpu.VMEM((spread_rows, PAIR), f32)],
         compiler_params=params,
-        cost_estimate=cost(0, 6 * blocks * tile_bytes),
+        cost_estimate=cost(0, 5 * blocks * tile_bytes),
         name="combine",
-    )(home, summed, odq)
-    mine = lax.all_to_all(results, "head", split_axis=0, concat_axis=0, tiled=True)
+    )(home, summed)
+    dkv = lax.all_to_all(dkv, "head", split_axis=0, concat_axis=0, tiled=True)
     return pl.pallas_call(
         unpack_kernel,
         out_shape=tuple(jax.ShapeDtypeStruct(queries.shape, bf) for _ in range(4)),
-        in_specs=[VMEM],
+        in_specs=[SMEM, ANY, VMEM],
         out_specs=(VMEM,) * 4,
-        compiler_params=params,
+        scratch_shapes=[
+            pltpu.VMEM((blocks, *tile), bf),
+            pltpu.SemaphoreType.DMA((blocks,)),
+        ],
         cost_estimate=cost(0, 4 * blocks * tile_bytes),
         name="unpack",
-    )(mine)
+    )(own_index, all_odq, dkv)
 
 
 def solution(mesh):

time: 223 us -> 215 us (0.964)
  between operations: 0.8 us -> 14.2 us
  waiting for transfers between devices: 83.9 us -> 70.9 us
  blocking collectives: 61.1 us -> 49.9 us
  local copies, waits for them, and re-layouts: 8.54 us -> 5.11 us
  Pallas kernels: 17.8 us -> 21.1 us
  other arithmetic: 3.29 us -> 5.6 us
    all_to_all x1, waiting for transfers between devices: 27.8 us -> 16.5 us  [body(): near = lax.all_to_all(kv, 'head', split_axis=0, concat_axis=0, tiled=True)]
    all_to_all x1, blocking collectives: 35.5 us -> 24.3 us  [body(): dkv = lax.all_to_all(dkv, 'head', split_axis=0, concat_axis=0, tiled=True)]
    unnamed x26 -> x12, local copies, waits for them, and re-layouts: 7.72 us -> 4.29 us
  transfers between devices with their start and end apart: 4 -> 6, of which waited for: 4 -> 4; matrix products, arithmetic and copies ran while one was open for 2% -> 3% of each run, Pallas kernels for 0% -> 3%
where the time goes in v3:
time: 215 us; the launch traced here: 214 us
  waiting for transfers between devices  70.9 us (33%)
  blocking collectives  49.9 us (23%)
  starting transfers between devices  46.7 us (22%)
  Pallas kernels  21.1 us (10%)
  between operations  14.2 us (7%)
  other arithmetic  5.6 us (3%)
  local copies, waits for them, and re-layouts  5.11 us (2%)
    all_to_all x1, blocking collectives, body(): lax.all_to_all(summed, 'slab', split_axis=0, concat_axis=0, tiled=True)  25.6 us
    all_to_all x1, blocking collectives, body(): dkv = lax.all_to_all(dkv, 'head', split_axis=0, concat_axis=0, tiled=True)  24.3 us
    all_to_all x1, waiting for transfers between devices, body(): lax.all_to_all(chosen, 'slab', split_axis=0, concat_axis=0, tiled=True)  21.4 us
    all_to_all x1, waiting for transfers between devices, body(): lax.all_to_all(far_out, 'slab', split_axis=0, concat_axis=0, tiled=True)  19.2 us
    all_to_all x1, starting transfers between devices, body(): near = lax.all_to_all(kv, 'head', split_axis=0, concat_axis=0, tiled=True)  18.2 us
    all_to_all x1, waiting for transfers between devices, body(): near = lax.all_to_all(kv, 'head', split_axis=0, concat_axis=0, tiled=True)  16.5 us
    all_to_all x1, waiting for transfers between devices, body(): lax.all_to_all(pieces, 'slab', split_axis=0, concat_axis=0, tiled=True)  13.8 us
    all_to_all x1, starting transfers between devices, body(): lax.all_to_all(pieces, 'slab', split_axis=0, concat_axis=0, tiled=True)  13.5 us
  transfers between devices with their start and end apart: 6, of which 4 were waited for; matrix products, arithmetic and copies ran while one was open for 3% of the time, Pallas kernels for 3%

profile of v3, /device:TPU:1, one launch (start us, length us, event | category | flops | bytes accessed | tf_op | source)
XLA Modules:
  0.0 213.5 jit_solution(5176622227971890469)
XLA Ops:
  7.2 2.3 %pack.1 = (bf16[16,128,128]{2,1,0:T(8,128)(2,1)}, bf16[16,128,128]{2,1,0:T(8,128)(2,1)}) custom-call(bf16[128,1024]{1,0:T(8,128)(2,1)} %k_ref.1, bf16[128,1024]{1,0:T(8,128)(2,1)} %v_ref.1, bf16[128,1024]{1,0:T(8,128)(2,1)} %q_ref.1, bf16[128,1024]{1,0:T(8,128)(2,1)} %g_ref.1), custom_call_target="tpu_custom_call" | custom-call | bytes 2097152 | tf_op jit(solution)/shard_map/pack/pallas_call | solution.py:269
  9.6 18.2 %all-to-all-start = ((bf16[16,128,128]{2,1,0:T(8,128)(2,1)}), bf16[16,128,128]{2,1,0:T(8,128)(2,1)S(1)}, u32[]{:S(2)}, u32[]{:S(2)}) async-start(bf16[16,128,128]{2,1,0:T(8,128)(2,1)} %get-tuple-element.9), calls=%async_computation | async-start | bytes 1048576 | tf_op jit(solution)/shard_map/all_to_all | solution.py:281
  27.8 0.8 slice_add_fusion
  28.6 16.5 %all-to-all-done.near_ref = bf16[16,128,128]{2,1,0:T(8,128)(2,1)S(1)} async-done(((bf16[16,128,128]{2,1,0:T(8,128)(2,1)}), bf16[16,128,128]{2,1,0:T(8,128)(2,1)S(1)}, u32[]{:S(2)}, u32[]{:S(2)}) %all-to-all-start) | async-done | bytes 524320 | tf_op jit(solution)/shard_map/all_to_all | solution.py:281
  45.1 1.9 spread.1
  47.0 13.5 %all-to-all-start.1 = ((bf16[64,32,128]{2,1,0:T(8,128)(2,1)}), bf16[64,32,128]{2,1,0:T(8,128)(2,1)}, u32[]{:S(2)}, u32[]{:S(2)}) async-start(bf16[64,32,128]{2,1,0:T(8,128)(2,1)} %bitcast.3), calls=%async_computation.1 | async-start | bytes 1048576 | tf_op jit(solution)/shard_map/all_to_all | solution.py:294
  60.5 2.1 select_reduce_fusion
  62.9 0.8 compare_and_fusion
  64.6 13.8 %all-to-all-done.1 = bf16[64,32,128]{2,1,0:T(8,128)(2,1)} async-done(((bf16[64,32,128]{2,1,0:T(8,128)(2,1)}), bf16[64,32,128]{2,1,0:T(8,128)(2,1)}, u32[]{:S(2)}, u32[]{:S(2)}) %all-to-all-start.1) | async-done | bytes 524320 | tf_op jit(solution)/shard_map/all_to_all | solution.py:294
  78.4 2.0 gather.1
  80.5 1.0 copy-done.2
  81.4 6.2 %all-to-all-start.2 = ((bf16[64,48,128]{2,1,0:T(8,128)(2,1)}), bf16[64,48,128]{2,1,0:T(8,128)(2,1)S(1)}, u32[]{:S(2)}, u32[]{:S(2)}) async-start(bf16[64,48,128]{2,1,0:T(8,128)(2,1)} %bitcast.18), calls=%async_computation.2 | async-start | bytes 1572864 | tf_op jit(solution)/shard_map/all_to_all | solution.py:305
  88.0 21.4 %all-to-all-done.2 = bf16[64,48,128]{2,1,0:T(8,128)(2,1)S(1)} async-done(((bf16[64,48,128]{2,1,0:T(8,128)(2,1)}), bf16[64,48,128]{2,1,0:T(8,128)(2,1)S(1)}, u32[]{:S(2)}, u32[]{:S(2)}) %all-to-all-start.2) | async-done | bytes 786464 | tf_op jit(solution)/shard_map/all_to_all | solution.py:305
  109.4 1.0 copy-done.1
  110.4 8.7 %attend.1 = (bf16[16,128,128]{2,1,0:T(8,128)(2,1)}, f32[16,128,128]{2,1,0:T(8,128)S(1)}, bf16[3072,128]{1,0:T(8,128)(2,1)}) custom-call(s32[1]{0:T(128)} %bitcast.index_ref, s32[40,2]{1,0:T(8,128)S(1)} %copy.29.links_ref, bf16[16,128,128]{2,1,0:T(8,128)(2,1)S(1)} %copy-done.1, bf16[3072,128]{1,0:T(8,128)(2,1)S(1)} %bitcast.17, ...), custom_call_target="tpu_custom_call" | custom-call | flops 1006632960 | bytes 3670016 | tf_op jit(solution)/shard_map/attend/pallas_call | solution.py:307
  119.1 1.1 copy-done.3
  120.2 8.7 %all-to-all-start.3 = ((bf16[64,48,128]{2,1,0:T(8,128)(2,1)}), bf16[64,48,128]{2,1,0:T(8,128)(2,1)}, u32[]{:S(2)}, u32[]{:S(2)}) async-start(bf16[64,48,128]{2,1,0:T(8,128)(2,1)} %bitcast.9), calls=%async_computation.3 | async-start | bytes 1572864 | tf_op jit(solution)/shard_map/all_to_all | solution.py:340
  129.0 1.3 fusion.1.hot_ref
  130.2 19.2 %all-to-all-done.3 = bf16[64,48,128]{2,1,0:T(8,128)(2,1)} async-done(((bf16[64,48,128]{2,1,0:T(8,128)(2,1)}), bf16[64,48,128]{2,1,0:T(8,128)(2,1)}, u32[]{:S(2)}, u32[]{:S(2)}) %all-to-all-start.3) | async-done | bytes 786464 | tf_op jit(solution)/shard_map/all_to_all | solution.py:340
  149.4 2.1 reduce.1
  151.5 25.6 %all_to_all.54 = bf16[64,32,128]{2,1,0:T(8,128)(2,1)S(1)} all-to-all(bf16[64,32,128]{2,1,0:T(8,128)(2,1)S(1)} %bitcast.19), channel_id=1, replica_groups=mesh['slab'=64,'head'=16] {'slab'}, dimensions={0} | all-to-all | bytes 1048576 | tf_op jit(solution)/shard_map/all_to_all | solution.py:354
  177.1 1.2 copy-done.4
  179.1 24.3 %all_to_all.55.dkv_ref = bf16[16,128,128]{2,1,0:T(8,128)(2,1)} all-to-all(bf16[16,128,128]{2,1,0:T(8,128)(2,1)S(1)} %combine.1), channel_id=1, replica_groups=mesh['slab'=64,'head'=16] {'head'}, dimensions={0} | all-to-all | bytes 1048576 | tf_op jit(solution)/shard_map/all_to_all | solution.py:365
  203.4 3.3 %unpack.1 = (bf16[128,1024]{1,0:T(8,128)(2,1)}, bf16[128,1024]{1,0:T(8,128)(2,1)}, bf16[128,1024]{1,0:T(8,128)(2,1)}, bf16[128,1024]{1,0:T(8,128)(2,1)}) custom-call(s32[1]{0:T(128)} %bitcast.index_ref, bf16[16,16,128,128]{3,2,1,0:T(8,128)(2,1)} %bitcast.22, bf16[16,128,128]{2,1,0:T(8,128)(2,1)} %all_to_all.55.dkv_ref), custom_call_target="tpu_custom_call" | custom-call | bytes 2097152 | tf_op jit(solution)/shard_map/unpack/pallas_call | solution.py:366
  (28 shorter events, 2.3 us)
Async XLA Ops:
  7.2 102.2 %all-gather.5.cloned.1.call-start = ((), (), s32[]{:S(2)}) async-start(), calls=%async_computation.6 | async-start | bytes 8912896 | tf_op jit(solution)/shard_map/all_gather | solution.py:282
  9.6 78.1 %copy-start.5 = (s32[64,40,2]{0,2,1:T(2,128)S(1)}, s32[64,40,2]{0,2,1:T(2,128)}, u32[]{:S(2)}) copy-start(s32[64,40,2]{0,2,1:T(2,128)} %param.10) | copy-start | bytes 61444
  9.6 35.5 %all-to-all-start = ((bf16[16,128,128]{2,1,0:T(8,128)(2,1)}), bf16[16,128,128]{2,1,0:T(8,128)(2,1)S(1)}, u32[]{:S(2)}, u32[]{:S(2)}) async-start(bf16[16,128,128]{2,1,0:T(8,128)(2,1)} %get-tuple-element.9), calls=%async_computation | async-start | bytes 1048576 | tf_op jit(solution)/shard_map/all_to_all | solution.py:281
  45.1 18.9 %copy-start = (bf16[16,128,128]{2,1,0:T(8,128)(2,1)}, bf16[16,128,128]{2,1,0:T(8,128)(2,1)S(1)}, u32[]{:S(2)}) copy-start(bf16[16,128,128]{2,1,0:T(8,128)(2,1)S(1)} %all-to-all-done.near_ref) | copy-start | bytes 1572868
  47.0 31.4 %all-to-all-start.1 = ((bf16[64,32,128]{2,1,0:T(8,128)(2,1)}), bf16[64,32,128]{2,1,0:T(8,128)(2,1)}, u32[]{:S(2)}, u32[]{:S(2)}) async-start(bf16[64,32,128]{2,1,0:T(8,128)(2,1)} %bitcast.3), calls=%async_computation.1 | async-start | bytes 1048576 | tf_op jit(solution)/shard_map/all_to_all | solution.py:294
  80.5 1.0 copy-start.2
  81.4 28.0 %all-to-all-start.2 = ((bf16[64,48,128]{2,1,0:T(8,128)(2,1)}), bf16[64,48,128]{2,1,0:T(8,128)(2,1)S(1)}, u32[]{:S(2)}, u32[]{:S(2)}) async-start(bf16[64,48,128]{2,1,0:T(8,128)(2,1)} %bitcast.18), calls=%async_computation.2 | async-start | bytes 1572864 | tf_op jit(solution)/shard_map/all_to_all | solution.py:305
  87.6 115.8 %all-gather.7.cloned.1.call-start = ((), (), s32[]{:S(2)}) async-start(), calls=%async_computation.7 | async-start | bytes 8912896 | tf_op jit(solution)/shard_map/all_gather | solution.py:338
  109.4 1.0 copy-start.1
  119.1 1.1 copy-start.3
  120.2 29.2 %all-to-all-start.3 = ((bf16[64,48,128]{2,1,0:T(8,128)(2,1)}), bf16[64,48,128]{2,1,0:T(8,128)(2,1)}, u32[]{:S(2)}, u32[]{:S(2)}) async-start(bf16[64,48,128]{2,1,0:T(8,128)(2,1)} %bitcast.9), calls=%async_computation.3 | async-start | bytes 1572864 | tf_op jit(solution)/shard_map/all_to_all | solution.py:340
  177.1 1.2 copy-start.4
Sparse Core Ops, SparseCore 0:
  10.7 75.8 all-gather.4
  120.4 56.2 all-gather.6

commit v4 on v3

--- a/solution.py
+++ b/solution.py
@@ -12,6 +12,7 @@
 BLK = 128
 PAIR = 2 * HD
 UNROLL = 8
+FEW = 16
 LIMIT = 48 * 1024 * 1024
 
 VMEM = pl.BlockSpec(memory_space=pltpu.VMEM)
@@ -240,9 +241,27 @@
 def body(queries, keys, values, out_grad, links, wanted):
     slabs = lax.axis_size("slab")
     blocks = lax.axis_size("head")
+    extra = links.shape[1] - blocks
+    named = links[:, blocks:, 1] - blocks
+    hit = named[:, :, None] == jnp.arange(slabs, dtype=jnp.int32)
+    used = jnp.any(hit & (links[:, blocks:, :1] >= 0), 1)
+    most = jnp.max(jnp.sum(used.astype(jnp.int32), 1))
+    given = (queries, keys, values, out_grad, used, links, wanted)
+    if extra <= FEW:
+        return step(*given, extra=extra)
+    return lax.cond(
+        most <= FEW,
+        functools.partial(step, extra=FEW),
+        functools.partial(step, extra=extra),
+        *given,
+    )
+
+
+def step(queries, keys, values, out_grad, used, links, wanted, *, extra):
+    slabs = lax.axis_size("slab")
+    blocks = lax.axis_size("head")
     slab_index = lax.axis_index("slab")
     link_count = links.shape[1]
-    extra = link_count - blocks
     parts = BLK // slabs
     bf, f32 = jnp.bfloat16, jnp.float32
     params = pltpu.CompilerParams(vmem_limit_bytes=LIMIT)
@@ -251,18 +270,23 @@
     sizes = dict(slabs=slabs, blocks=blocks, extra=extra)
     spread_rows, far_rows = slabs * parts * blocks, slabs * parts * extra
 
-    slots = links[:, blocks:, 1]
-    named = slots - blocks
-    hit = named[:, :, None] == jnp.arange(slabs, dtype=jnp.int32)
-    block_named = jnp.sum(jnp.where(hit, wanted[:, None, :], 0), -1)
-    is_far = (named >= 0) & (links[:, blocks:, 0] >= 0)
-    piece = jnp.where(is_far, named * blocks + block_named, -1).reshape(-1)
+    slab_ids = jnp.arange(slabs, dtype=jnp.int32)
+    before = (slab_ids[:, None] < slab_ids[None, :]).astype(bf)
+    place = jnp.dot(used.astype(bf), before, preferred_element_type=f32).astype(jnp.int32)
+    places = jnp.arange(extra, dtype=jnp.int32)
+    at = used[:, None, :] & (place[:, None, :] == places[None, :, None])
+    row = slab_ids[None, :] * blocks + wanted
+    piece = jnp.sum(jnp.where(at, row[:, None, :] + 1, 0), -1).reshape(-1) - 1
     all_pieces = jnp.arange(slabs * blocks, dtype=jnp.int32)
     hot = (piece[:, None] == all_pieces[None, :]).astype(bf)
     hot_turned = (all_pieces[:, None] == piece[None, :]).astype(bf)
     own_links = lax.dynamic_index_in_dim(links, slab_index, 0, keepdims=False)
-    link_ids = jnp.arange(link_count, dtype=jnp.int32)
-    own_slots = jnp.where(own_links[:, 1] >= blocks, link_ids, own_links[:, 1])
+    own_place = lax.dynamic_index_in_dim(place, slab_index, 0, keepdims=False)
+    own_named = own_links[:, 1] - blocks
+    own_place = jnp.sum(jnp.where(own_named[:, None] == slab_ids, own_place, 0), -1)
+    own_slots = jnp.where(
+        own_named >= 0, blocks + jnp.minimum(own_place, extra - 1), own_links[:, 1]
+    )
     own_links = jnp.stack([own_links[:, 0], own_slots], -1)
 
     own_index = lax.axis_index("head").astype(jnp.int32).reshape(1)
@@ -314,7 +338,7 @@
         in_specs=[SMEM, SMEM, VMEM, VMEM, ANY],
         out_specs=(VMEM, VMEM, VMEM),
         scratch_shapes=[
-            pltpu.VMEM((link_count, *tile), bf),
+            pltpu.VMEM((blocks + extra, *tile), bf),
             pltpu.VMEM((blocks, 2 * BLK, PAIR), bf),
             pltpu.VMEM((link_count, BLK, BLK), f32),
             pltpu.VMEM((link_count, BLK, BLK), f32),
@@ -322,7 +346,7 @@
             pltpu.VMEM((blocks, 1, BLK), f32),
             pltpu.VMEM((blocks, 1, BLK), f32),
             pltpu.VMEM((blocks, PAIR, BLK), f32),
-            pltpu.VMEM((link_count, *tile), f32),
+            pltpu.VMEM((blocks + extra, *tile), f32),
             pltpu.VMEM((far_rows, PAIR), f32),
             pltpu.VMEM((blocks, *tile), bf),
             pltpu.SemaphoreType.DMA((blocks,)),

time: 215 us -> 217 us (level)
    unnamed x12 -> x0, local copies, waits for them, and re-layouts: 4.29 us -> none
    cond x0 -> x12, local copies, waits for them, and re-layouts: none -> 3.09 us
  transfers between devices with their start and end apart: 6 -> 6, of which waited for: 4 -> 4; matrix products, arithmetic and copies ran while one was open for 3% -> 2% of each run, Pallas kernels for 3% -> 3%
where the time goes in v4:
time: 217 us; the launch traced here: 216 us
  waiting for transfers between devices  72.9 us (34%)
  blocking collectives  49.9 us (23%)
  starting transfers between devices  46.7 us (22%)
  Pallas kernels  21.2 us (10%)
  between operations  14.7 us (7%)
  other arithmetic  6.14 us (3%)
  local copies, waits for them, and re-layouts  3.56 us (2%)
    all_to_all x1, blocking collectives, step(): lax.all_to_all(summed, 'slab', split_axis=0, concat_axis=0, tiled=True)  25.6 us
    all_to_all x1, blocking collectives, step(): dkv = lax.all_to_all(dkv, 'head', split_axis=0, concat_axis=0, tiled=True)  24.4 us
    all_to_all x1, waiting for transfers between devices, step(): lax.all_to_all(chosen, 'slab', split_axis=0, concat_axis=0, tiled=True)  21.2 us
    all_to_all x1, waiting for transfers between devices, step(): lax.all_to_all(far_out, 'slab', split_axis=0, concat_axis=0, tiled=True)  19.2 us
    all_to_all x1, starting transfers between devices, step(): near = lax.all_to_all(kv, 'head', split_axis=0, concat_axis=0, tiled=True)  18.2 us
    all_to_all x1, waiting for transfers between devices, step(): near = lax.all_to_all(kv, 'head', split_axis=0, concat_axis=0, tiled=True)  16.5 us
    all_to_all x1, waiting for transfers between devices, step(): lax.all_to_all(pieces, 'slab', split_axis=0, concat_axis=0, tiled=True)  15.9 us
    all_to_all x1, starting transfers between devices, step(): lax.all_to_all(pieces, 'slab', split_axis=0, concat_axis=0, tiled=True)  13.5 us
  transfers between devices with their start and end apart: 6, of which 4 were waited for; matrix products, arithmetic and copies ran while one was open for 2% of the time, Pallas kernels for 3%

profile of v4, /device:TPU:1, one launch (start us, length us, event | category | flops | bytes accessed | tf_op | source)
XLA Modules:
  0.0 215.7 jit_solution(1170615185070839328)
XLA Ops:
  7.2 0.8 fusion.10
  10.2 198.6 %conditional.1 = ((bf16[128,1024]{1,0:T(8,128)(2,1)}, bf16[128,1024]{1,0:T(8,128)(2,1)}, bf16[128,1024]{1,0:T(8,128)(2,1)}, bf16[128,1024]{1,0:T(8,128)(2,1)})) conditional(s32[]{:T(128)} %convert_element_type.35, (s32[64,40,2]{0,2,1:T(2,128)}, pred[64,64]{1,0:T(8,128)(4,1)S(1)}, bf16[128,1024]{1,0:T(8,128)(2,1)}, bf16[128,1024]{1,0:T(8,128)(2,1)}, ...), branch_computations={%region_3.6_spmd, %region_6.9_spmd} | conditional | flops 2624479232 | bytes 104641536 | solution.py:252
  10.3 2.3 %pack.2 = (bf16[16,128,128]{2,1,0:T(8,128)(2,1)}, bf16[16,128,128]{2,1,0:T(8,128)(2,1)}) custom-call(bf16[128,1024]{1,0:T(8,128)(2,1)} %get-tuple-element.30.k_ref, bf16[128,1024]{1,0:T(8,128)(2,1)} %get-tuple-element.31.v_ref, bf16[128,1024]{1,0:T(8,128)(2,1)} %get-tuple-element.32.q_ref, bf16[128,1024]{1,0:T(8,128)(2,1)} %get-tuple-element.33.g_ref), custom_call_target="tpu_custom_call" | custom-call | bytes 2097152 | tf_op jit(solution)/shard_map/cond/branch_0_fun/pack/pallas_call | solution.py:293
  12.6 18.2 %all-to-all-start = ((bf16[16,128,128]{2,1,0:T(8,128)(2,1)}), bf16[16,128,128]{2,1,0:T(8,128)(2,1)S(1)}, u32[]{:S(2)}, u32[]{:S(2)}) async-start(bf16[16,128,128]{2,1,0:T(8,128)(2,1)} %get-tuple-element.34), calls=%async_computation | async-start | bytes 1048576 | tf_op jit(solution)/shard_map/cond/branch_0_fun/all_to_all | solution.py:305
  30.8 0.8 add_add_fusion
  31.6 16.5 %all-to-all-done.near_ref = bf16[16,128,128]{2,1,0:T(8,128)(2,1)S(1)} async-done(((bf16[16,128,128]{2,1,0:T(8,128)(2,1)}), bf16[16,128,128]{2,1,0:T(8,128)(2,1)S(1)}, u32[]{:S(2)}, u32[]{:S(2)}) %all-to-all-start) | async-done | bytes 524320 | tf_op jit(solution)/shard_map/cond/branch_0_fun/all_to_all | solution.py:305
  48.1 1.9 spread.2
  50.0 13.5 %all-to-all-start.1 = ((bf16[64,32,128]{2,1,0:T(8,128)(2,1)}), bf16[64,32,128]{2,1,0:T(8,128)(2,1)}, u32[]{:S(2)}, u32[]{:S(2)}) async-start(bf16[64,32,128]{2,1,0:T(8,128)(2,1)} %bitcast.6), calls=%async_computation.1 | async-start | bytes 1048576 | tf_op jit(solution)/shard_map/cond/branch_0_fun/all_to_all | solution.py:318
  63.6 1.2 select_reduce_fusion
  65.5 15.9 %all-to-all-done.1 = bf16[64,32,128]{2,1,0:T(8,128)(2,1)} async-done(((bf16[64,32,128]{2,1,0:T(8,128)(2,1)}), bf16[64,32,128]{2,1,0:T(8,128)(2,1)}, u32[]{:S(2)}, u32[]{:S(2)}) %all-to-all-start.1) | async-done | bytes 524320 | tf_op jit(solution)/shard_map/cond/branch_0_fun/all_to_all | solution.py:318
  81.4 2.0 gather.2
  83.5 1.0 copy-done.3
  84.4 6.2 %all-to-all-start.2 = ((bf16[64,48,128]{2,1,0:T(8,128)(2,1)}), bf16[64,48,128]{2,1,0:T(8,128)(2,1)S(1)}, u32[]{:S(2)}, u32[]{:S(2)}) async-start(bf16[64,48,128]{2,1,0:T(8,128)(2,1)} %bitcast.47), calls=%async_computation.2 | async-start | bytes 1572864 | tf_op jit(solution)/shard_map/cond/branch_0_fun/all_to_all | solution.py:329
  91.1 21.2 %all-to-all-done.2 = bf16[64,48,128]{2,1,0:T(8,128)(2,1)S(1)} async-done(((bf16[64,48,128]{2,1,0:T(8,128)(2,1)}), bf16[64,48,128]{2,1,0:T(8,128)(2,1)S(1)}, u32[]{:S(2)}, u32[]{:S(2)}) %all-to-all-start.2) | async-done | bytes 786464 | tf_op jit(solution)/shard_map/cond/branch_0_fun/all_to_all | solution.py:329
  112.4 1.0 copy-done.2
  113.4 8.7 %attend.2 = (bf16[16,128,128]{2,1,0:T(8,128)(2,1)}, f32[16,128,128]{2,1,0:T(8,128)S(1)}, bf16[3072,128]{1,0:T(8,128)(2,1)}) custom-call(s32[1]{0:T(128)} %bitcast.index_ref, s32[40,2]{1,0:T(8,128)S(1)} %copy.46.links_ref, bf16[16,128,128]{2,1,0:T(8,128)(2,1)S(1)} %copy-done.2, bf16[3072,128]{1,0:T(8,128)(2,1)S(1)} %bitcast.46, ...), custom_call_target="tpu_custom_call" | custom-call | flops 1006632960 | bytes 3670016 | tf_op jit(solution)/shard_map/cond/branch_0_fun/attend/pallas_call | solution.py:331
  122.1 1.1 copy-done.5
  123.2 8.8 %all-to-all-start.3 = ((bf16[64,48,128]{2,1,0:T(8,128)(2,1)}), bf16[64,48,128]{2,1,0:T(8,128)(2,1)}, u32[]{:S(2)}, u32[]{:S(2)}) async-start(bf16[64,48,128]{2,1,0:T(8,128)(2,1)} %bitcast.12), calls=%async_computation.3 | async-start | bytes 1572864 | tf_op jit(solution)/shard_map/cond/branch_0_fun/all_to_all | solution.py:364
  132.0 1.3 fusion.1.hot_ref
  133.2 19.2 %all-to-all-done.3 = bf16[64,48,128]{2,1,0:T(8,128)(2,1)} async-done(((bf16[64,48,128]{2,1,0:T(8,128)(2,1)}), bf16[64,48,128]{2,1,0:T(8,128)(2,1)}, u32[]{:S(2)}, u32[]{:S(2)}) %all-to-all-start.3) | async-done | bytes 786464 | tf_op jit(solution)/shard_map/cond/branch_0_fun/all_to_all | solution.py:364
  152.4 2.2 %reduce.2 = bf16[2048,128]{1,0:T(8,128)(2,1)S(1)} custom-call(bf16[1024,1536]{1,0:T(8,128)(2,1)S(1)} %fusion.1.hot_ref, bf16[3072,128]{1,0:T(8,128)(2,1)} %bitcast.13.in_ref), custom_call_target="tpu_custom_call" | custom-call | flops 805306368 | bytes 2621440 | tf_op jit(solution)/shard_map/cond/branch_0_fun/reduce/pallas_call | solution.py:365
  154.7 25.6 %all_to_all.80 = bf16[64,32,128]{2,1,0:T(8,128)(2,1)S(1)} all-to-all(bf16[64,32,128]{2,1,0:T(8,128)(2,1)S(1)} %bitcast.49), channel_id=1, replica_groups=mesh['slab'=64,'head'=16] {'slab'}, dimensions={0} | all-to-all | bytes 1048576 | tf_op jit(solution)/shard_map/cond/branch_0_fun/all_to_all | solution.py:378
  181.0 24.4 %all_to_all.81.dkv_ref = bf16[16,128,128]{2,1,0:T(8,128)(2,1)} all-to-all(bf16[16,128,128]{2,1,0:T(8,128)(2,1)S(1)} %combine.2), channel_id=1, replica_groups=mesh['slab'=64,'head'=16] {'head'}, dimensions={0} | all-to-all | bytes 1048576 | tf_op jit(solution)/shard_map/cond/branch_0_fun/all_to_all | solution.py:389
  205.3 3.3 %unpack.2 = (bf16[128,1024]{1,0:T(8,128)(2,1)}, bf16[128,1024]{1,0:T(8,128)(2,1)}, bf16[128,1024]{1,0:T(8,128)(2,1)}, bf16[128,1024]{1,0:T(8,128)(2,1)}) custom-call(s32[1]{0:T(128)} %bitcast.index_ref, bf16[16,16,128,128]{3,2,1,0:T(8,128)(2,1)} %bitcast.59, bf16[16,128,128]{2,1,0:T(8,128)(2,1)} %all_to_all.81.dkv_ref), custom_call_target="tpu_custom_call" | custom-call | bytes 2097152 | tf_op jit(solution)/shard_map/cond/branch_0_fun/unpack/pallas_call | solution.py:390
  (35 shorter events, 3.6 us)
Async XLA Ops:
  10.2 102.1 %all-gather.9.cloned.1.call-start = ((), (), s32[]{:S(2)}) async-start(), calls=%async_computation.12 | async-start | bytes 8912896 | tf_op jit(solution)/shard_map/cond/branch_0_fun/all_gather | solution.py:306
  12.6 35.5 %all-to-all-start = ((bf16[16,128,128]{2,1,0:T(8,128)(2,1)}), bf16[16,128,128]{2,1,0:T(8,128)(2,1)S(1)}, u32[]{:S(2)}, u32[]{:S(2)}) async-start(bf16[16,128,128]{2,1,0:T(8,128)(2,1)} %get-tuple-element.34), calls=%async_computation | async-start | bytes 1048576 | tf_op jit(solution)/shard_map/cond/branch_0_fun/all_to_all | solution.py:305
  48.1 16.7 %copy-start.1 = (bf16[16,128,128]{2,1,0:T(8,128)(2,1)}, bf16[16,128,128]{2,1,0:T(8,128)(2,1)S(1)}, u32[]{:S(2)}) copy-start(bf16[16,128,128]{2,1,0:T(8,128)(2,1)S(1)} %all-to-all-done.near_ref) | copy-start | bytes 1572868 | tf_op jit(solution)/shard_map/cond
  50.0 31.4 %all-to-all-start.1 = ((bf16[64,32,128]{2,1,0:T(8,128)(2,1)}), bf16[64,32,128]{2,1,0:T(8,128)(2,1)}, u32[]{:S(2)}, u32[]{:S(2)}) async-start(bf16[64,32,128]{2,1,0:T(8,128)(2,1)} %bitcast.6), calls=%async_computation.1 | async-start | bytes 1048576 | tf_op jit(solution)/shard_map/cond/branch_0_fun/all_to_all | solution.py:318
  64.9 25.8 %copy-start.11 = (s32[64,40,2]{0,2,1:T(2,128)S(1)}, s32[64,40,2]{0,2,1:T(2,128)}, u32[]{:S(2)}) copy-start(s32[64,40,2]{0,2,1:T(2,128)} %get-tuple-element.110) | copy-start | bytes 61444 | tf_op jit(solution)/shard_map/cond
  83.4 1.0 copy-start.3
  84.4 27.9 %all-to-all-start.2 = ((bf16[64,48,128]{2,1,0:T(8,128)(2,1)}), bf16[64,48,128]{2,1,0:T(8,128)(2,1)S(1)}, u32[]{:S(2)}, u32[]{:S(2)}) async-start(bf16[64,48,128]{2,1,0:T(8,128)(2,1)} %bitcast.47), calls=%async_computation.2 | async-start | bytes 1572864 | tf_op jit(solution)/shard_map/cond/branch_0_fun/all_to_all | solution.py:329
  90.6 114.7 %all-gather.11.cloned.1.call-start = ((), (), s32[]{:S(2)}) async-start(), calls=%async_computation.13 | async-start | bytes 8912896 | tf_op jit(solution)/shard_map/cond/branch_0_fun/all_gather | solution.py:362
  112.4 1.0 copy-start.2
  122.1 1.1 copy-start.5
  123.2 29.2 %all-to-all-start.3 = ((bf16[64,48,128]{2,1,0:T(8,128)(2,1)}), bf16[64,48,128]{2,1,0:T(8,128)(2,1)}, u32[]{:S(2)}, u32[]{:S(2)}) async-start(bf16[64,48,128]{2,1,0:T(8,128)(2,1)} %bitcast.12), calls=%async_computation.3 | async-start | bytes 1572864 | tf_op jit(solution)/shard_map/cond/branch_0_fun/all_to_all | solution.py:364
  152.4 27.8 %copy-start.6 = (f32[16,128,128]{2,1,0:T(8,128)S(1)}, f32[16,128,128]{2,1,0:T(8,128)}, u32[]{:S(2)}) copy-start(f32[16,128,128]{2,1,0:T(8,128)} %copy-done.5) | copy-start | bytes 3145732 | tf_op jit(solution)/shard_map/cond
Sparse Core Ops, SparseCore 0:
  13.7 75.7 all-gather.8
  123.3 56.2 all-gather.10

commit v5 on v4

--- a/solution.py
+++ b/solution.py
@@ -12,8 +12,10 @@
 BLK = 128
 PAIR = 2 * HD
 UNROLL = 8
+OTHER_UNROLL = 12
 FEW = 16
 LIMIT = 48 * 1024 * 1024
+ATTEND_LIMIT = 60 * 1024 * 1024
 
 VMEM = pl.BlockSpec(memory_space=pltpu.VMEM)
 SMEM = pl.BlockSpec(memory_space=pltpu.SMEM)
@@ -24,13 +26,27 @@
     return pl.CostEstimate(flops=flops, bytes_accessed=moved, transcendentals=exps)
 
 
-def pack_kernel(k_ref, v_ref, q_ref, g_ref, kv_ref, qg_ref, held, sems):
+def most_far(links_ref, blocks):
+    queried, slots = links_ref[blocks:, 0, :], links_ref[blocks:, 1, :]
+    order = lax.broadcasted_iota(jnp.int32, slots.shape, 0)
+    far = (queried >= 0) & (slots >= blocks)
+    keys = jnp.where(far, slots, -1 - order)
+    total = far[:1].astype(jnp.float32)
+    for p in range(1, slots.shape[0]):
+        same = (keys[:p] == keys[p : p + 1]).astype(jnp.float32)
+        again = jnp.max(same, axis=0, keepdims=True)
+        total = total + far[p : p + 1].astype(jnp.float32) * (1.0 - again)
+    return jnp.max(total).astype(jnp.int32)
+
+
+def pack_kernel(links_ref, k_ref, v_ref, q_ref, g_ref, kv_ref, qg_ref, most_ref, held, sems):
     copies = [
         pltpu.make_async_copy(ref, held.at[i], sems.at[i])
         for i, ref in enumerate((k_ref, v_ref, q_ref, g_ref))
     ]
     for copy in copies:
         copy.start()
+    most_ref[0] = most_far(links_ref, kv_ref.shape[0])
     for first, out_ref in ((0, kv_ref), (2, qg_ref)):
         copies[first].wait()
         copies[first + 1].wait()
@@ -46,19 +62,27 @@
     ]
 
 
-def unpack_kernel(index_ref, odq_ref, dkv_ref, o_ref, dq_ref, dk_ref, dv_ref, held, sems):
+def unpack_kernel(
+    index_ref, odq_ref, dkv_ref, o_ref, dq_ref, dk_ref, dv_ref, held, rows, sems, out_sems
+):
     copies = own_tiles(odq_ref, index_ref[0], held, sems)
     for copy in copies:
         copy.start()
-    for tiles, first_ref, second_ref in ((dkv_ref, dk_ref, dv_ref), (held, dq_ref, o_ref)):
+    outs = []
+    for tiles, first, out_refs in ((dkv_ref, 0, (dk_ref, dv_ref)), (held, 2, (dq_ref, o_ref))):
         if tiles is held:
             for copy in copies:
                 copy.wait()
         for h in range(0, tiles.shape[0], 2):
             even, odd = tiles[h], tiles[h + 1]
             cols = slice(h * HD, (h + 2) * HD)
-            first_ref[:, cols] = jnp.concatenate([even[:, :HD], odd[:, :HD]], axis=1)
-            second_ref[:, cols] = jnp.concatenate([even[:, HD:], odd[:, HD:]], axis=1)
+            rows[first, :, cols] = jnp.concatenate([even[:, :HD], odd[:, :HD]], axis=1)
+            rows[first + 1, :, cols] = jnp.concatenate([even[:, HD:], odd[:, HD:]], axis=1)
+        for i, out_ref in enumerate(out_refs, first):
+            outs.append(pltpu.make_async_copy(rows.at[i], out_ref, out_sems.at[i]))
+            outs[-1].start()
+    for out in outs:
+        out.wait()
 
 
 def each_piece(slabs, held):
@@ -159,11 +183,7 @@
         table[blocks + p, rows, :] = wide[piece_rows, :].astype(jnp.bfloat16)
     for b in range(blocks):
         table[b] = near_ref[b]
-    top[...] = jnp.full_like(top, -3e38)
-    total[...] = jnp.zeros_like(total)
-    delta[...] = jnp.zeros_like(delta)
-    acc[...] = jnp.zeros_like(acc)
-    dkv[...] = jnp.zeros_like(dkv)
+    dkv[blocks:] = jnp.zeros((slots - blocks, BLK, PAIR), jnp.float32)
     for copy in copies:
         copy.wait()
     for b in range(blocks):
@@ -172,14 +192,16 @@
         masked[b, BLK:, :] = jnp.where(left, jnp.zeros_like(own), own)
 
     def each_link(step):
-        def group(i, _):
-            for r in range(UNROLL):
-                j = i * UNROLL + r
+        def other(i, _):
+            for r in range(OTHER_UNROLL):
+                j = blocks + i * OTHER_UNROLL + r
                 queried = links_ref[j, 0]
                 step(j, jnp.maximum(queried, 0), links_ref[j, 1], queried >= 0)
             return 0
 
-        lax.fori_loop(0, link_count // UNROLL, group, 0)
+        for b in range(blocks):
+            step(b, b, b, None)
+        lax.fori_loop(0, (link_count - blocks) // OTHER_UNROLL, other, 0)
 
     def score_step(j, b, s, valid):
         both = lax.dot_general(
@@ -188,14 +210,19 @@
         s_buf[j] = both[:, :BLK]
         d_buf[j] = both[:, BLK:]
         largest = jnp.max(both[:, :BLK], axis=0, keepdims=True)
-        top[b] = jnp.maximum(top[b], jnp.where(valid, largest, -3e38))
+        if valid is None:
+            top[b] = largest
+        else:
+            top[b] = jnp.maximum(top[b], jnp.where(valid, largest, -3e38))
 
     def sum_step(j, b, s, valid):
-        shift = top[b] + jnp.where(valid, 0.0, 1e30)
+        shift = top[b] if valid is None else top[b] + jnp.where(valid, 0.0, 1e30)
         raised = jnp.exp2((s_buf[j] - shift) * exp_scale)
         s_buf[j] = raised
-        total[b] = total[b] + jnp.sum(raised, axis=0, keepdims=True)
-        delta[b] = delta[b] + jnp.sum(raised * d_buf[j], axis=0, keepdims=True)
+        part = jnp.sum(raised, axis=0, keepdims=True)
+        weighted = jnp.sum(raised * d_buf[j], axis=0, keepdims=True)
+        total[b] = part if valid is None else total[b] + part
+        delta[b] = weighted if valid is None else delta[b] + weighted
 
     def grad_step(j, b, s, valid):
         prob = (s_buf[j] * total[b]).astype(jnp.bfloat16)
@@ -208,14 +235,20 @@
             (((0,), (0,)), ((), ())),
             preferred_element_type=jnp.float32,
         )
-        acc[b, :HD, :] += turned[:HD, BLK:]
-        acc[b, HD:, :] += turned[HD:, :BLK]
         terms = jnp.dot(
             jnp.concatenate([dscore, prob], axis=0),
             qg[b],
             preferred_element_type=jnp.float32,
         )
-        dkv[s] += jnp.where(left, terms[:BLK], terms[BLK:])
+        both = jnp.where(left, terms[:BLK], terms[BLK:])
+        if valid is None:
+            acc[b, :HD, :] = turned[:HD, BLK:]
+            acc[b, HD:, :] = turned[HD:, :BLK]
+            dkv[s] = both
+        else:
+            acc[b, :HD, :] += turned[:HD, BLK:]
+            acc[b, HD:, :] += turned[HD:, :BLK]
+            dkv[s] += both
 
     each_link(score_step)
     each_link(sum_step)
@@ -232,35 +265,51 @@
     home_ref[...] = dkv[:blocks]
 
 
-def combine_kernel(home_ref, returned_ref, out_ref, wide, *, slabs):
+def combine_kernel(home_ref, returned_ref, out_ref, wide, home, sem, *, slabs):
+    copy = pltpu.make_async_copy(home_ref, home, sem)
+    copy.start()
     wide[...] = returned_ref[...].astype(jnp.float32)
-    for c, rows, piece_rows in each_piece(slabs, home_ref.shape[0]):
-        out_ref[c, rows, :] = (home_ref[c, rows, :] + wide[piece_rows, :]).astype(jnp.bfloat16)
+    copy.wait()
+    for c, rows, piece_rows in each_piece(slabs, home.shape[0]):
+        out_ref[c, rows, :] = (home[c, rows, :] + wide[piece_rows, :]).astype(jnp.bfloat16)
 
 
 def body(queries, keys, values, out_grad, links, wanted):
-    slabs = lax.axis_size("slab")
     blocks = lax.axis_size("head")
     extra = links.shape[1] - blocks
-    named = links[:, blocks:, 1] - blocks
-    hit = named[:, :, None] == jnp.arange(slabs, dtype=jnp.int32)
-    used = jnp.any(hit & (links[:, blocks:, :1] >= 0), 1)
-    most = jnp.max(jnp.sum(used.astype(jnp.int32), 1))
-    given = (queries, keys, values, out_grad, used, links, wanted)
+    bf = jnp.bfloat16
+    kv, qg, most = pl.pallas_call(
+        pack_kernel,
+        out_shape=(
+            jax.ShapeDtypeStruct((blocks, BLK, PAIR), bf),
+            jax.ShapeDtypeStruct((blocks, BLK, PAIR), bf),
+            jax.ShapeDtypeStruct((1,), jnp.int32),
+        ),
+        in_specs=[VMEM] + [ANY] * 4,
+        out_specs=(VMEM, VMEM, SMEM),
+        scratch_shapes=[
+            pltpu.VMEM((4, *queries.shape), bf),
+            pltpu.SemaphoreType.DMA((4,)),
+        ],
+        cost_estimate=cost(0, 16 * blocks * BLK * PAIR),
+        name="pack",
+    )(links.transpose(1, 2, 0), keys, values, queries, out_grad)
+    given = (kv, qg, links, wanted)
     if extra <= FEW:
         return step(*given, extra=extra)
     return lax.cond(
-        most <= FEW,
+        most[0] <= FEW,
         functools.partial(step, extra=FEW),
         functools.partial(step, extra=extra),
         *given,
     )
 
 
-def step(queries, keys, values, out_grad, used, links, wanted, *, extra):
+def step(kv, qg, links, wanted, *, extra):
     slabs = lax.axis_size("slab")
     blocks = lax.axis_size("head")
     slab_index = lax.axis_index("slab")
+    own_index = lax.axis_index("head").astype(jnp.int32).reshape(1)
     link_count = links.shape[1]
     parts = BLK // slabs
     bf, f32 = jnp.bfloat16, jnp.float32
@@ -270,6 +319,9 @@
     sizes = dict(slabs=slabs, blocks=blocks, extra=extra)
     spread_rows, far_rows = slabs * parts * blocks, slabs * parts * extra
 
+    named = links[:, blocks:, 1] - blocks
+    hit = named[:, :, None] == jnp.arange(slabs, dtype=jnp.int32)
+    used = jnp.any(hit & (links[:, blocks:, :1] >= 0), 1)
     slab_ids = jnp.arange(slabs, dtype=jnp.int32)
     before = (slab_ids[:, None] < slab_ids[None, :]).astype(bf)
     place = jnp.dot(used.astype(bf), before, preferred_element_type=f32).astype(jnp.int32)
@@ -279,7 +331,6 @@
     piece = jnp.sum(jnp.where(at, row[:, None, :] + 1, 0), -1).reshape(-1) - 1
     all_pieces = jnp.arange(slabs * blocks, dtype=jnp.int32)
     hot = (piece[:, None] == all_pieces[None, :]).astype(bf)
-    hot_turned = (all_pieces[:, None] == piece[None, :]).astype(bf)
     own_links = lax.dynamic_index_in_dim(links, slab_index, 0, keepdims=False)
     own_place = lax.dynamic_index_in_dim(place, slab_index, 0, keepdims=False)
     own_named = own_links[:, 1] - blocks
@@ -289,19 +340,6 @@
     )
     own_links = jnp.stack([own_links[:, 0], own_slots], -1)
 
-    own_index = lax.axis_index("head").astype(jnp.int32).reshape(1)
-    kv, qg = pl.pallas_call(
-        pack_kernel,
-        out_shape=(jax.ShapeDtypeStruct((blocks, *tile), bf),) * 2,
-        in_specs=[ANY] * 4,
-        out_specs=(VMEM,) * 2,
-        scratch_shapes=[
-            pltpu.VMEM((4, *queries.shape), bf),
-            pltpu.SemaphoreType.DMA((4,)),
-        ],
-        cost_estimate=cost(0, 4 * blocks * tile_bytes),
-        name="pack",
-    )(keys, values, queries, out_grad)
     near = lax.all_to_all(kv, "head", split_axis=0, concat_axis=0, tiled=True)
     all_qg = lax.all_gather(qg, "head")
 
@@ -316,6 +354,7 @@
         name="spread",
     )(near)
     pieces = lax.all_to_all(pieces, "slab", split_axis=0, concat_axis=0, tiled=True)
+    pieces, own_links = lax.optimization_barrier((pieces, own_links))
     chosen = pl.pallas_call(
         functools.partial(gather_kernel, **sizes),
         out_shape=jax.ShapeDtypeStruct((far_rows, PAIR), bf),
@@ -351,7 +390,7 @@
             pltpu.VMEM((blocks, *tile), bf),
             pltpu.SemaphoreType.DMA((blocks,)),
         ],
-        compiler_params=params,
+        compiler_params=pltpu.CompilerParams(vmem_limit_bytes=ATTEND_LIMIT),
         cost_estimate=cost(
             link_count * 6 * BLK * BLK * PAIR * 2,
             (2 * extra + 4 * blocks) * tile_bytes,
@@ -361,6 +400,8 @@
     )(own_index, own_links, near, far, all_qg)
     all_odq = lax.all_gather(odq, "head")
 
+    far_out, piece = lax.optimization_barrier((far_out, piece))
+    hot_turned = (all_pieces[:, None] == piece[None, :]).astype(bf)
     returned = lax.all_to_all(far_out, "slab", split_axis=0, concat_axis=0, tiled=True)
     summed = pl.pallas_call(
         functools.partial(reduce_kernel, **sizes),
@@ -379,9 +420,13 @@
     dkv = pl.pallas_call(
         functools.partial(combine_kernel, slabs=slabs),
         out_shape=jax.ShapeDtypeStruct((blocks, *tile), bf),
-        in_specs=[VMEM, VMEM],
+        in_specs=[ANY, VMEM],
         out_specs=VMEM,
-        scratch_shapes=[pltpu.VMEM((spread_rows, PAIR), f32)],
+        scratch_shapes=[
+            pltpu.VMEM((spread_rows, PAIR), f32),
+            pltpu.VMEM((blocks, *tile), f32),
+            pltpu.SemaphoreType.DMA,
+        ],
         compiler_params=params,
         cost_estimate=cost(0, 5 * blocks * tile_bytes),
         name="combine",
@@ -389,12 +434,14 @@
     dkv = lax.all_to_all(dkv, "head", split_axis=0, concat_axis=0, tiled=True)
     return pl.pallas_call(
         unpack_kernel,
-        out_shape=tuple(jax.ShapeDtypeStruct(queries.shape, bf) for _ in range(4)),
+        out_shape=tuple(jax.ShapeDtypeStruct((BLK, blocks * HD), bf) for _ in range(4)),
         in_specs=[SMEM, ANY, VMEM],
-        out_specs=(VMEM,) * 4,
+        out_specs=(ANY,) * 4,
         scratch_shapes=[
             pltpu.VMEM((blocks, *tile), bf),
+            pltpu.VMEM((4, BLK, blocks * HD), bf),
             pltpu.SemaphoreType.DMA((blocks,)),
+            pltpu.SemaphoreType.DMA((4,)),
         ],
         cost_estimate=cost(0, 4 * blocks * tile_bytes),
         name="unpack",

time: 217 us -> 199 us (0.917)
  waiting for transfers between devices: 72.9 us -> 63.5 us
  Pallas kernels: 21.2 us -> 18.8 us
    all_to_all x1, waiting for transfers between devices: 21.2 us -> 16.5 us  [step(): lax.all_to_all(chosen, 'slab', split_axis=0, concat_axis=0, tiled=True)]
    all_to_all x1, waiting for transfers between devices: 19.2 us -> 15.4 us  [step(): lax.all_to_all(far_out, 'slab', split_axis=0, concat_axis=0, tiled=True)]
    all_to_all x1, waiting for transfers between devices: 16.5 us -> 13.4 us  [step(): near = lax.all_to_all(kv, 'head', split_axis=0, concat_axis=0, tiled=True)]
    all_to_all x1, blocking collectives: 25.6 us -> 23.3 us  [step(): lax.all_to_all(summed, 'slab', split_axis=0, concat_axis=0, tiled=True)]
  transfers between devices with their start and end apart: 6 -> 6, of which waited for: 4 -> 4; matrix products, arithmetic and copies ran while one was open for 2% -> 3% of each run, Pallas kernels for 3% -> 2%
where the time goes in v5:
time: 199 us; the launch traced here: 198 us
  waiting for transfers between devices  63.5 us (32%)
  blocking collectives  48.1 us (24%)
  starting transfers between devices  45 us (23%)
  Pallas kernels  18.8 us (9%)
  between operations  14.7 us (7%)
  other arithmetic  4.01 us (2%)
  local copies, waits for them, and re-layouts  3.57 us (2%)
    all_to_all x1, blocking collectives, step(): dkv = lax.all_to_all(dkv, 'head', split_axis=0, concat_axis=0, tiled=True)  24.8 us
    all_to_all x1, blocking collectives, step(): lax.all_to_all(summed, 'slab', split_axis=0, concat_axis=0, tiled=True)  23.3 us
    all_to_all x1, starting transfers between devices, step(): near = lax.all_to_all(kv, 'head', split_axis=0, concat_axis=0, tiled=True)  18.2 us
    all_to_all x1, waiting for transfers between devices, step(): lax.all_to_all(pieces, 'slab', split_axis=0, concat_axis=0, tiled=True)  17.4 us
    all_to_all x1, waiting for transfers between devices, step(): lax.all_to_all(chosen, 'slab', split_axis=0, concat_axis=0, tiled=True)  16.5 us
    all_to_all x1, waiting for transfers between devices, step(): lax.all_to_all(far_out, 'slab', split_axis=0, concat_axis=0, tiled=True)  15.4 us
    all_to_all x1, waiting for transfers between devices, step(): near = lax.all_to_all(kv, 'head', split_axis=0, concat_axis=0, tiled=True)  13.4 us
    all_to_all x1, starting transfers between devices, step(): lax.all_to_all(pieces, 'slab', split_axis=0, concat_axis=0, tiled=True)  13.2 us
  transfers between devices with their start and end apart: 6, of which 4 were waited for; matrix products, arithmetic and copies ran while one was open for 3% of the time, Pallas kernels for 2%

profile of v5, /device:TPU:1, one launch (start us, length us, event | category | flops | bytes accessed | tf_op | source)
XLA Modules:
  0.0 198.2 jit_solution(17502091387445245700)
XLA Ops:
  7.2 3.1 %pack.1 = (bf16[16,128,128]{2,1,0:T(8,128)(2,1)}, bf16[16,128,128]{2,1,0:T(8,128)(2,1)}, s32[1]{0:T(128)}) custom-call(s32[40,2,64]{2,1,0:T(2,128)} %bitcast.62, bf16[128,1024]{1,0:T(8,128)(2,1)} %k_ref.1, bf16[128,1024]{1,0:T(8,128)(2,1)} %v_ref.1, bf16[128,1024]{1,0:T(8,128)(2,1)} %q_ref.1, bf16[128,1024]{1,0:T(8,128)(2,1)} %g_ref.1), custom_call_target="tpu_custom_call" | custom-call | bytes 4194304 | tf_op jit(solution)/shard_map/pack/pallas_call | solution.py:281
  10.9 180.4 %conditional.1 = ((bf16[128,1024]{1,0:T(8,128)(2,1)}, bf16[128,1024]{1,0:T(8,128)(2,1)}, bf16[128,1024]{1,0:T(8,128)(2,1)}, bf16[128,1024]{1,0:T(8,128)(2,1)})) conditional(s32[]{:T(128)} %bitcast.33, (bf16[16,128,128]{2,1,0:T(8,128)(2,1)}, s32[64,40,2]{0,2,1:T(2,128)}, s32[64,64]{1,0:T(8,128)}, bf16[16,128,128]{2,1,0:T(8,128)(2,1)}) %tuple.17, ...), branch_computations={%region_0.4_spmd, %region_4.8_spmd} | conditional | flops 2624773120 | bytes 97219520 | solution.py:300
  11.9 18.2 %all-to-all-start.6 = ((bf16[16,128,128]{2,1,0:T(8,128)(2,1)}), bf16[16,128,128]{2,1,0:T(8,128)(2,1)S(1)}, u32[]{:S(2)}, u32[]{:S(2)}) async-start(bf16[16,128,128]{2,1,0:T(8,128)(2,1)} %get-tuple-element.27), calls=%async_computation.6 | async-start | bytes 1048576 | tf_op jit(solution)/shard_map/cond/branch_1_fun/all_to_all | solution.py:343
  30.1 0.8 copy.67
  31.8 0.8 add_add_fusion.1
  32.6 1.2 select_reduce_fusion.2
  34.0 13.4 %all-to-all-done.6.near_ref = bf16[16,128,128]{2,1,0:T(8,128)(2,1)S(1)} async-done(((bf16[16,128,128]{2,1,0:T(8,128)(2,1)}), bf16[16,128,128]{2,1,0:T(8,128)(2,1)S(1)}, u32[]{:S(2)}, u32[]{:S(2)}) %all-to-all-start.6) | async-done | bytes 524320 | tf_op jit(solution)/shard_map/cond/branch_1_fun/all_to_all | solution.py:343
  47.4 1.9 spread.3
  49.3 13.2 %all-to-all-start.7 = ((bf16[64,32,128]{2,1,0:T(8,128)(2,1)}), bf16[64,32,128]{2,1,0:T(8,128)(2,1)S(1)}, u32[]{:S(2)}, u32[]{:S(2)}) async-start(bf16[64,32,128]{2,1,0:T(8,128)(2,1)} %bitcast.17), calls=%async_computation.7 | async-start | bytes 1048576 | tf_op jit(solution)/shard_map/cond/branch_1_fun/all_to_all | solution.py:356
  63.2 17.4 %all-to-all-done.7 = bf16[64,32,128]{2,1,0:T(8,128)(2,1)S(1)} async-done(((bf16[64,32,128]{2,1,0:T(8,128)(2,1)}), bf16[64,32,128]{2,1,0:T(8,128)(2,1)S(1)}, u32[]{:S(2)}, u32[]{:S(2)}) %all-to-all-start.7) | async-done | bytes 524320 | tf_op jit(solution)/shard_map/cond/branch_1_fun/all_to_all | solution.py:356
  80.6 0.7 gather.3
  81.4 0.8 copy-done.3
  82.2 6.3 %all-to-all-start.8 = ((bf16[64,32,128]{2,1,0:T(8,128)(2,1)}), bf16[64,32,128]{2,1,0:T(8,128)(2,1)S(1)}, u32[]{:S(2)}, u32[]{:S(2)}) async-start(bf16[64,32,128]{2,1,0:T(8,128)(2,1)} %bitcast.49), calls=%async_computation.8 | async-start | bytes 1048576 | tf_op jit(solution)/shard_map/cond/branch_1_fun/all_to_all | solution.py:368
  89.3 16.5 %all-to-all-done.8 = bf16[64,32,128]{2,1,0:T(8,128)(2,1)S(1)} async-done(((bf16[64,32,128]{2,1,0:T(8,128)(2,1)}), bf16[64,32,128]{2,1,0:T(8,128)(2,1)S(1)}, u32[]{:S(2)}, u32[]{:S(2)}) %all-to-all-start.8) | async-done | bytes 524320 | tf_op jit(solution)/shard_map/cond/branch_1_fun/all_to_all | solution.py:368
  105.8 0.8 copy-done.7
  106.6 8.3 %attend.3 = (bf16[16,128,128]{2,1,0:T(8,128)(2,1)}, f32[16,128,128]{2,1,0:T(8,128)}, bf16[2048,128]{1,0:T(8,128)(2,1)}) custom-call(s32[1]{0:T(128)} %bitcast.16.index_ref, s32[40,2]{1,0:T(8,128)} %copy.65.links_ref, bf16[16,128,128]{2,1,0:T(8,128)(2,1)} %copy-done.1, bf16[2048,128]{1,0:T(8,128)(2,1)} %bitcast.59, bf16[16,16,128,128]{3,2,1,0:T(8,128)(2,1)} %bitcast.55), custom_call_target="tpu_custom_call" | custom-call | flops 1006632960 | bytes 3145728 | tf_op jit(solution)/shard_map/cond/branch_1_fun/attend/pallas_call | solution.py:370
  114.9 7.2 %all-to-all-start.9 = ((bf16[64,32,128]{2,1,0:T(8,128)(2,1)}), bf16[64,32,128]{2,1,0:T(8,128)(2,1)S(1)}, u32[]{:S(2)}, u32[]{:S(2)}) async-start(bf16[64,32,128]{2,1,0:T(8,128)(2,1)} %bitcast.61), calls=%async_computation.9 | async-start | bytes 1048576 | tf_op jit(solution)/shard_map/cond/branch_1_fun/all_to_all | solution.py:405
  122.1 0.9 fusion.8.hot_ref
  123.0 15.4 %all-to-all-done.9 = bf16[64,32,128]{2,1,0:T(8,128)(2,1)S(1)} async-done(((bf16[64,32,128]{2,1,0:T(8,128)(2,1)}), bf16[64,32,128]{2,1,0:T(8,128)(2,1)S(1)}, u32[]{:S(2)}, u32[]{:S(2)}) %all-to-all-start.9) | async-done | bytes 524320 | tf_op jit(solution)/shard_map/cond/branch_1_fun/all_to_all | solution.py:405
  138.4 0.7 reduce.7
  139.2 23.3 %all_to_all.84 = bf16[64,32,128]{2,1,0:T(8,128)(2,1)S(1)} all-to-all(bf16[64,32,128]{2,1,0:T(8,128)(2,1)S(1)} %bitcast.53), channel_id=1, replica_groups=mesh['slab'=64,'head'=16] {'slab'}, dimensions={0} | all-to-all | bytes 1048576 | tf_op jit(solution)/shard_map/cond/branch_1_fun/all_to_all | solution.py:419
  162.4 0.8 combine.3
  163.2 24.8 %all_to_all.85.dkv_ref = bf16[16,128,128]{2,1,0:T(8,128)(2,1)} all-to-all(bf16[16,128,128]{2,1,0:T(8,128)(2,1)S(1)} %combine.3), channel_id=1, replica_groups=mesh['slab'=64,'head'=16] {'head'}, dimensions={0} | all-to-all | bytes 1048576 | tf_op jit(solution)/shard_map/cond/branch_1_fun/all_to_all | solution.py:434
  188.1 3.2 %unpack.3 = (bf16[128,1024]{1,0:T(8,128)(2,1)}, bf16[128,1024]{1,0:T(8,128)(2,1)}, bf16[128,1024]{1,0:T(8,128)(2,1)}, bf16[128,1024]{1,0:T(8,128)(2,1)}) custom-call(s32[1]{0:T(128)} %bitcast.16.index_ref, bf16[16,16,128,128]{3,2,1,0:T(8,128)(2,1)} %bitcast.57, bf16[16,128,128]{2,1,0:T(8,128)(2,1)} %all_to_all.85.dkv_ref), custom_call_target="tpu_custom_call" | custom-call | bytes 2097152 | tf_op jit(solution)/shard_map/cond/branch_1_fun/unpack/pallas_call | solution.py:435
  (29 shorter events, 3.3 us)
Async XLA Ops:
  11.1 94.7 %all-gather.13.cloned.1.call-start = ((), (), s32[]{:S(2)}) async-start(), calls=%async_computation.14 | async-start | bytes 8912896 | tf_op jit(solution)/shard_map/cond/branch_1_fun/all_gather | solution.py:344
  11.9 35.5 %all-to-all-start.6 = ((bf16[16,128,128]{2,1,0:T(8,128)(2,1)}), bf16[16,128,128]{2,1,0:T(8,128)(2,1)S(1)}, u32[]{:S(2)}, u32[]{:S(2)}) async-start(bf16[16,128,128]{2,1,0:T(8,128)(2,1)} %get-tuple-element.27), calls=%async_computation.6 | async-start | bytes 1048576 | tf_op jit(solution)/shard_map/cond/branch_1_fun/all_to_all | solution.py:343
  47.4 34.8 %copy-start.1 = (bf16[16,128,128]{2,1,0:T(8,128)(2,1)}, bf16[16,128,128]{2,1,0:T(8,128)(2,1)S(1)}, u32[]{:S(2)}) copy-start(bf16[16,128,128]{2,1,0:T(8,128)(2,1)S(1)} %all-to-all-done.6.near_ref) | copy-start | bytes 1572868 | tf_op jit(solution)/shard_map/cond
  49.3 31.3 %all-to-all-start.7 = ((bf16[64,32,128]{2,1,0:T(8,128)(2,1)}), bf16[64,32,128]{2,1,0:T(8,128)(2,1)S(1)}, u32[]{:S(2)}, u32[]{:S(2)}) async-start(bf16[64,32,128]{2,1,0:T(8,128)(2,1)} %bitcast.17), calls=%async_computation.7 | async-start | bytes 1048576 | tf_op jit(solution)/shard_map/cond/branch_1_fun/all_to_all | solution.py:356
  81.3 0.8 copy-start.3
  82.2 23.6 %all-to-all-start.8 = ((bf16[64,32,128]{2,1,0:T(8,128)(2,1)}), bf16[64,32,128]{2,1,0:T(8,128)(2,1)S(1)}, u32[]{:S(2)}, u32[]{:S(2)}) async-start(bf16[64,32,128]{2,1,0:T(8,128)(2,1)} %bitcast.49), calls=%async_computation.8 | async-start | bytes 1048576 | tf_op jit(solution)/shard_map/cond/branch_1_fun/all_to_all | solution.py:368
  88.5 99.6 %all-gather.15.cloned.1.call-start = ((), (), s32[]{:S(2)}) async-start(), calls=%async_computation.15 | async-start | bytes 8912896 | tf_op jit(solution)/shard_map/cond/branch_1_fun/all_gather | solution.py:401
  105.8 0.8 copy-start.7
  114.9 23.5 %all-to-all-start.9 = ((bf16[64,32,128]{2,1,0:T(8,128)(2,1)}), bf16[64,32,128]{2,1,0:T(8,128)(2,1)S(1)}, u32[]{:S(2)}, u32[]{:S(2)}) async-start(bf16[64,32,128]{2,1,0:T(8,128)(2,1)} %bitcast.61), calls=%async_computation.9 | async-start | bytes 1048576 | tf_op jit(solution)/shard_map/cond/branch_1_fun/all_to_all | solution.py:405
  138.4 24.0 %copy-start.5 = (f32[16,128,128]{2,1,0:T(8,128)S(1)}, f32[16,128,128]{2,1,0:T(8,128)}, u32[]{:S(2)}) copy-start(f32[16,128,128]{2,1,0:T(8,128)} %get-tuple-element.34.home_ref) | copy-start | bytes 3145732 | tf_op jit(solution)/shard_map/cond
Sparse Core Ops, SparseCore 0:
  14.7 75.7 all-gather.12
  115.1 54.9 all-gather.14

commit v6 on v5

--- a/solution.py
+++ b/solution.py
@@ -12,7 +12,7 @@
 BLK = 128
 PAIR = 2 * HD
 UNROLL = 8
-OTHER_UNROLL = 12
+OTHER_UNROLL = 24
 FEW = 16
 LIMIT = 48 * 1024 * 1024
 ATTEND_LIMIT = 60 * 1024 * 1024
@@ -63,16 +63,16 @@
 
 
 def unpack_kernel(
-    index_ref, odq_ref, dkv_ref, o_ref, dq_ref, dk_ref, dv_ref, held, rows, sems, out_sems
+    index_ref, odq_ref, dkv_ref, o_ref, dq_ref, dk_ref, dv_ref, held, dkv, rows, sems, dkv_sem, out_sems
 ):
+    dkv_copy = pltpu.make_async_copy(dkv_ref, dkv, dkv_sem)
     copies = own_tiles(odq_ref, index_ref[0], held, sems)
-    for copy in copies:
+    for copy in (dkv_copy, *copies):
         copy.start()
     outs = []
-    for tiles, first, out_refs in ((dkv_ref, 0, (dk_ref, dv_ref)), (held, 2, (dq_ref, o_ref))):
-        if tiles is held:
-            for copy in copies:
-                copy.wait()
+    for tiles, first, out_refs in ((dkv, 0, (dk_ref, dv_ref)), (held, 2, (dq_ref, o_ref))):
+        for copy in copies if tiles is held else (dkv_copy,):
+            copy.wait()
         for h in range(0, tiles.shape[0], 2):
             even, odd = tiles[h], tiles[h + 1]
             cols = slice(h * HD, (h + 2) * HD)
@@ -166,14 +166,16 @@
     wide,
     qg,
     sems,
+    near_sem,
     *,
     slabs,
 ):
+    blocks, slots = near_ref.shape[0], table.shape[0]
+    link_count = links_ref.shape[0] // 2
     copies = own_tiles(all_qg_ref, index_ref[0], qg, sems)
+    copies.append(pltpu.make_async_copy(near_ref, table.at[pl.ds(0, blocks)], near_sem))
     for copy in copies:
         copy.start()
-    blocks, slots = near_ref.shape[0], table.shape[0]
-    link_count = links_ref.shape[0]
     score_scale = 1.0 / math.sqrt(HD)
     exp_scale = score_scale * math.log2(math.e)
     left = lax.broadcasted_iota(jnp.int32, (BLK, PAIR), 1) < HD
@@ -181,8 +183,6 @@
     wide[...] = far_ref[...].astype(jnp.float32)
     for p, rows, piece_rows in each_piece(slabs, slots - blocks):
         table[blocks + p, rows, :] = wide[piece_rows, :].astype(jnp.bfloat16)
-    for b in range(blocks):
-        table[b] = near_ref[b]
     dkv[blocks:] = jnp.zeros((slots - blocks, BLK, PAIR), jnp.float32)
     for copy in copies:
         copy.wait()
@@ -195,8 +195,8 @@
         def other(i, _):
             for r in range(OTHER_UNROLL):
                 j = blocks + i * OTHER_UNROLL + r
-                queried = links_ref[j, 0]
-                step(j, jnp.maximum(queried, 0), links_ref[j, 1], queried >= 0)
+                queried = links_ref[2 * j]
+                step(j, jnp.maximum(queried, 0), links_ref[2 * j + 1], queried >= 0)
             return 0
 
         for b in range(blocks):
@@ -338,7 +338,7 @@
     own_slots = jnp.where(
         own_named >= 0, blocks + jnp.minimum(own_place, extra - 1), own_links[:, 1]
     )
-    own_links = jnp.stack([own_links[:, 0], own_slots], -1)
+    own_links = jnp.stack([own_links[:, 0], own_slots], -1).reshape(-1)
 
     near = lax.all_to_all(kv, "head", split_axis=0, concat_axis=0, tiled=True)
     all_qg = lax.all_gather(qg, "head")
@@ -374,7 +374,7 @@
             jax.ShapeDtypeStruct((blocks, *tile), f32),
             jax.ShapeDtypeStruct((far_rows, PAIR), bf),
         ),
-        in_specs=[SMEM, SMEM, VMEM, VMEM, ANY],
+        in_specs=[SMEM, SMEM, ANY, VMEM, ANY],
         out_specs=(VMEM, VMEM, VMEM),
         scratch_shapes=[
             pltpu.VMEM((blocks + extra, *tile), bf),
@@ -389,6 +389,7 @@
             pltpu.VMEM((far_rows, PAIR), f32),
             pltpu.VMEM((blocks, *tile), bf),
             pltpu.SemaphoreType.DMA((blocks,)),
+            pltpu.SemaphoreType.DMA,
         ],
         compiler_params=pltpu.CompilerParams(vmem_limit_bytes=ATTEND_LIMIT),
         cost_estimate=cost(
@@ -435,12 +436,14 @@
     return pl.pallas_call(
         unpack_kernel,
         out_shape=tuple(jax.ShapeDtypeStruct((BLK, blocks * HD), bf) for _ in range(4)),
-        in_specs=[SMEM, ANY, VMEM],
+        in_specs=[SMEM, ANY, ANY],
         out_specs=(ANY,) * 4,
         scratch_shapes=[
             pltpu.VMEM((blocks, *tile), bf),
+            pltpu.VMEM((blocks, *tile), bf),
             pltpu.VMEM((4, BLK, blocks * HD), bf),
             pltpu.SemaphoreType.DMA((blocks,)),
+            pltpu.SemaphoreType.DMA,
             pltpu.SemaphoreType.DMA((4,)),
         ],
         cost_estimate=cost(0, 4 * blocks * tile_bytes),

time: 199 us -> 199 us (level)
    all_to_all x1, waiting for transfers between devices: 17.4 us -> 14.9 us  [step(): lax.all_to_all(pieces, 'slab', split_axis=0, concat_axis=0, tiled=True)]
where the time goes in v6:
time: 199 us; the launch traced here: 198 us
  waiting for transfers between devices  63.2 us (32%)
  blocking collectives  48.1 us (24%)
  starting transfers between devices  45.2 us (23%)
  Pallas kernels  18.2 us (9%)
  between operations  14.7 us (7%)
  other arithmetic  4.01 us (2%)
  local copies, waits for them, and re-layouts  3.6 us (2%)
    all_to_all x1, blocking collectives, step(): dkv = lax.all_to_all(dkv, 'head', split_axis=0, concat_axis=0, tiled=True)  24.7 us
    all_to_all x1, blocking collectives, step(): lax.all_to_all(summed, 'slab', split_axis=0, concat_axis=0, tiled=True)  23.4 us
    all_to_all x1, starting transfers between devices, step(): near = lax.all_to_all(kv, 'head', split_axis=0, concat_axis=0, tiled=True)  18.2 us
    all_to_all x1, waiting for transfers between devices, step(): lax.all_to_all(chosen, 'slab', split_axis=0, concat_axis=0, tiled=True)  17.2 us
    all_to_all x1, waiting for transfers between devices, step(): near = lax.all_to_all(kv, 'head', split_axis=0, concat_axis=0, tiled=True)  15.2 us
    all_to_all x1, waiting for transfers between devices, step(): lax.all_to_all(far_out, 'slab', split_axis=0, concat_axis=0, tiled=True)  15.2 us
    all_to_all x1, waiting for transfers between devices, step(): lax.all_to_all(pieces, 'slab', split_axis=0, concat_axis=0, tiled=True)  14.9 us
    all_to_all x1, starting transfers between devices, step(): lax.all_to_all(pieces, 'slab', split_axis=0, concat_axis=0, tiled=True)  13.2 us
  transfers between devices with their start and end apart: 6, of which 4 were waited for; matrix products, arithmetic and copies ran while one was open for 3% of the time, Pallas kernels for 2%

profile of v6, /device:TPU:1, one launch (start us, length us, event | category | flops | bytes accessed | tf_op | source)
XLA Modules:
  0.0 197.9 jit_solution(11490486348238732774)
XLA Ops:
  7.2 3.1 %pack.1 = (bf16[16,128,128]{2,1,0:T(8,128)(2,1)}, bf16[16,128,128]{2,1,0:T(8,128)(2,1)}, s32[1]{0:T(128)}) custom-call(s32[40,2,64]{2,1,0:T(2,128)} %bitcast.62, bf16[128,1024]{1,0:T(8,128)(2,1)} %k_ref.1, bf16[128,1024]{1,0:T(8,128)(2,1)} %v_ref.1, bf16[128,1024]{1,0:T(8,128)(2,1)} %q_ref.1, bf16[128,1024]{1,0:T(8,128)(2,1)} %g_ref.1), custom_call_target="tpu_custom_call" | custom-call | bytes 4194304 | tf_op jit(solution)/shard_map/pack/pallas_call | solution.py:281
  10.9 180.1 %conditional.1 = ((bf16[128,1024]{1,0:T(8,128)(2,1)}, bf16[128,1024]{1,0:T(8,128)(2,1)}, bf16[128,1024]{1,0:T(8,128)(2,1)}, bf16[128,1024]{1,0:T(8,128)(2,1)})) conditional(s32[]{:T(128)} %bitcast.33, (bf16[16,128,128]{2,1,0:T(8,128)(2,1)}, s32[64,40,2]{0,2,1:T(2,128)}, s32[64,64]{1,0:T(8,128)}, bf16[16,128,128]{2,1,0:T(8,128)(2,1)}) %tuple.17, ...), branch_computations={%region_0.4_spmd, %region_4.8_spmd} | conditional | flops 2624773120 | bytes 97220160 | solution.py:300
  11.9 18.2 %all-to-all-start.6 = ((bf16[16,128,128]{2,1,0:T(8,128)(2,1)}), bf16[16,128,128]{2,1,0:T(8,128)(2,1)S(1)}, u32[]{:S(2)}, u32[]{:S(2)}) async-start(bf16[16,128,128]{2,1,0:T(8,128)(2,1)} %get-tuple-element.27), calls=%async_computation.6 | async-start | bytes 1048576 | tf_op jit(solution)/shard_map/cond/branch_1_fun/all_to_all | solution.py:343
  30.1 0.8 copy.55
  32.2 15.2 %all-to-all-done.6.near_ref = bf16[16,128,128]{2,1,0:T(8,128)(2,1)S(1)} async-done(((bf16[16,128,128]{2,1,0:T(8,128)(2,1)}), bf16[16,128,128]{2,1,0:T(8,128)(2,1)S(1)}, u32[]{:S(2)}, u32[]{:S(2)}) %all-to-all-start.6) | async-done | bytes 524320 | tf_op jit(solution)/shard_map/cond/branch_1_fun/all_to_all | solution.py:343
  47.4 1.9 spread.3
  49.3 13.2 %all-to-all-start.7 = ((bf16[64,32,128]{2,1,0:T(8,128)(2,1)}), bf16[64,32,128]{2,1,0:T(8,128)(2,1)S(1)}, u32[]{:S(2)}, u32[]{:S(2)}) async-start(bf16[64,32,128]{2,1,0:T(8,128)(2,1)} %bitcast.17), calls=%async_computation.7 | async-start | bytes 1048576 | tf_op jit(solution)/shard_map/cond/branch_1_fun/all_to_all | solution.py:356
  63.3 0.8 add_add_fusion.1
  64.1 1.2 select_reduce_fusion.2
  65.7 14.9 %all-to-all-done.7 = bf16[64,32,128]{2,1,0:T(8,128)(2,1)S(1)} async-done(((bf16[64,32,128]{2,1,0:T(8,128)(2,1)}), bf16[64,32,128]{2,1,0:T(8,128)(2,1)S(1)}, u32[]{:S(2)}, u32[]{:S(2)}) %all-to-all-start.7) | async-done | bytes 524320 | tf_op jit(solution)/shard_map/cond/branch_1_fun/all_to_all | solution.py:356
  80.6 0.7 gather.3
  81.4 0.8 copy-done.3
  82.2 6.3 %all-to-all-start.8 = ((bf16[64,32,128]{2,1,0:T(8,128)(2,1)}), bf16[64,32,128]{2,1,0:T(8,128)(2,1)S(1)}, u32[]{:S(2)}, u32[]{:S(2)}) async-start(bf16[64,32,128]{2,1,0:T(8,128)(2,1)} %bitcast.49), calls=%async_computation.8 | async-start | bytes 1048576 | tf_op jit(solution)/shard_map/cond/branch_1_fun/all_to_all | solution.py:368
  88.6 17.2 %all-to-all-done.8 = bf16[64,32,128]{2,1,0:T(8,128)(2,1)S(1)} async-done(((bf16[64,32,128]{2,1,0:T(8,128)(2,1)}), bf16[64,32,128]{2,1,0:T(8,128)(2,1)S(1)}, u32[]{:S(2)}, u32[]{:S(2)}) %all-to-all-start.8) | async-done | bytes 524320 | tf_op jit(solution)/shard_map/cond/branch_1_fun/all_to_all | solution.py:368
  105.8 0.8 copy-done.7
  106.6 8.2 %attend.3 = (bf16[16,128,128]{2,1,0:T(8,128)(2,1)}, f32[16,128,128]{2,1,0:T(8,128)}, bf16[2048,128]{1,0:T(8,128)(2,1)}) custom-call(s32[1]{0:T(128)} %bitcast.16.index_ref, s32[80]{0:T(128)} %reshape.103.links_ref, bf16[16,128,128]{2,1,0:T(8,128)(2,1)} %copy-done.1, bf16[2048,128]{1,0:T(8,128)(2,1)} %bitcast.59, bf16[16,16,128,128]{3,2,1,0:T(8,128)(2,1)} %bitcast.55), custom_call_target="tpu_custom_call" | custom-call | flops 1006632960 | bytes 3145728 | tf_op jit(solution)/shard_map/cond/branch_1_fun/attend/pallas_call | solution.py:370
  114.8 7.4 %all-to-all-start.9 = ((bf16[64,32,128]{2,1,0:T(8,128)(2,1)}), bf16[64,32,128]{2,1,0:T(8,128)(2,1)S(1)}, u32[]{:S(2)}, u32[]{:S(2)}) async-start(bf16[64,32,128]{2,1,0:T(8,128)(2,1)} %bitcast.61), calls=%async_computation.9 | async-start | bytes 1048576 | tf_op jit(solution)/shard_map/cond/branch_1_fun/all_to_all | solution.py:406
  122.2 0.9 fusion.8.hot_ref
  123.1 15.2 %all-to-all-done.9 = bf16[64,32,128]{2,1,0:T(8,128)(2,1)S(1)} async-done(((bf16[64,32,128]{2,1,0:T(8,128)(2,1)}), bf16[64,32,128]{2,1,0:T(8,128)(2,1)S(1)}, u32[]{:S(2)}, u32[]{:S(2)}) %all-to-all-start.9) | async-done | bytes 524320 | tf_op jit(solution)/shard_map/cond/branch_1_fun/all_to_all | solution.py:406
  138.3 0.7 reduce.7
  139.0 23.4 %all_to_all.84 = bf16[64,32,128]{2,1,0:T(8,128)(2,1)S(1)} all-to-all(bf16[64,32,128]{2,1,0:T(8,128)(2,1)S(1)} %bitcast.53), channel_id=1, replica_groups=mesh['slab'=64,'head'=16] {'slab'}, dimensions={0} | all-to-all | bytes 1048576 | tf_op jit(solution)/shard_map/cond/branch_1_fun/all_to_all | solution.py:420
  162.4 0.8 combine.3
  163.3 24.7 %all_to_all.85.dkv_ref = bf16[16,128,128]{2,1,0:T(8,128)(2,1)} all-to-all(bf16[16,128,128]{2,1,0:T(8,128)(2,1)S(1)} %combine.3), channel_id=1, replica_groups=mesh['slab'=64,'head'=16] {'head'}, dimensions={0} | all-to-all | bytes 1048576 | tf_op jit(solution)/shard_map/cond/branch_1_fun/all_to_all | solution.py:435
  188.0 2.8 %unpack.3 = (bf16[128,1024]{1,0:T(8,128)(2,1)}, bf16[128,1024]{1,0:T(8,128)(2,1)}, bf16[128,1024]{1,0:T(8,128)(2,1)}, bf16[128,1024]{1,0:T(8,128)(2,1)}) custom-call(s32[1]{0:T(128)} %bitcast.16.index_ref, bf16[16,16,128,128]{3,2,1,0:T(8,128)(2,1)} %bitcast.57, bf16[16,128,128]{2,1,0:T(8,128)(2,1)} %all_to_all.85.dkv_ref), custom_call_target="tpu_custom_call" | custom-call | bytes 2097152 | tf_op jit(solution)/shard_map/cond/branch_1_fun/unpack/pallas_call | solution.py:436
  (30 shorter events, 3.3 us)
Async XLA Ops:
  11.1 94.7 %all-gather.13.cloned.1.call-start = ((), (), s32[]{:S(2)}) async-start(), calls=%async_computation.14 | async-start | bytes 8912896 | tf_op jit(solution)/shard_map/cond/branch_1_fun/all_gather | solution.py:344
  11.9 35.5 %all-to-all-start.6 = ((bf16[16,128,128]{2,1,0:T(8,128)(2,1)}), bf16[16,128,128]{2,1,0:T(8,128)(2,1)S(1)}, u32[]{:S(2)}, u32[]{:S(2)}) async-start(bf16[16,128,128]{2,1,0:T(8,128)(2,1)} %get-tuple-element.27), calls=%async_computation.6 | async-start | bytes 1048576 | tf_op jit(solution)/shard_map/cond/branch_1_fun/all_to_all | solution.py:343
  47.4 34.8 %copy-start.1 = (bf16[16,128,128]{2,1,0:T(8,128)(2,1)}, bf16[16,128,128]{2,1,0:T(8,128)(2,1)S(1)}, u32[]{:S(2)}) copy-start(bf16[16,128,128]{2,1,0:T(8,128)(2,1)S(1)} %all-to-all-done.6.near_ref) | copy-start | bytes 1572868 | tf_op jit(solution)/shard_map/cond
  49.3 31.3 %all-to-all-start.7 = ((bf16[64,32,128]{2,1,0:T(8,128)(2,1)}), bf16[64,32,128]{2,1,0:T(8,128)(2,1)S(1)}, u32[]{:S(2)}, u32[]{:S(2)}) async-start(bf16[64,32,128]{2,1,0:T(8,128)(2,1)} %bitcast.17), calls=%async_computation.7 | async-start | bytes 1048576 | tf_op jit(solution)/shard_map/cond/branch_1_fun/all_to_all | solution.py:356
  81.3 0.8 copy-start.3
  82.2 23.6 %all-to-all-start.8 = ((bf16[64,32,128]{2,1,0:T(8,128)(2,1)}), bf16[64,32,128]{2,1,0:T(8,128)(2,1)S(1)}, u32[]{:S(2)}, u32[]{:S(2)}) async-start(bf16[64,32,128]{2,1,0:T(8,128)(2,1)} %bitcast.49), calls=%async_computation.8 | async-start | bytes 1048576 | tf_op jit(solution)/shard_map/cond/branch_1_fun/all_to_all | solution.py:368
  88.5 99.5 %all-gather.15.cloned.1.call-start = ((), (), s32[]{:S(2)}) async-start(), calls=%async_computation.15 | async-start | bytes 8912896 | tf_op jit(solution)/shard_map/cond/branch_1_fun/all_gather | solution.py:402
  105.8 0.8 copy-start.7
  114.8 23.5 %all-to-all-start.9 = ((bf16[64,32,128]{2,1,0:T(8,128)(2,1)}), bf16[64,32,128]{2,1,0:T(8,128)(2,1)S(1)}, u32[]{:S(2)}, u32[]{:S(2)}) async-start(bf16[64,32,128]{2,1,0:T(8,128)(2,1)} %bitcast.61), calls=%async_computation.9 | async-start | bytes 1048576 | tf_op jit(solution)/shard_map/cond/branch_1_fun/all_to_all | solution.py:406
  138.3 24.2 %copy-start.5 = (f32[16,128,128]{2,1,0:T(8,128)S(1)}, f32[16,128,128]{2,1,0:T(8,128)}, u32[]{:S(2)}) copy-start(f32[16,128,128]{2,1,0:T(8,128)} %get-tuple-element.34.home_ref) | copy-start | bytes 3145732 | tf_op jit(solution)/shard_map/cond
Sparse Core Ops, SparseCore 0:
  14.7 75.7 all-gather.12
  114.9 54.9 all-gather.14

commit v7 on v6

--- a/solution.py
+++ b/solution.py
@@ -39,20 +39,24 @@
     return jnp.max(total).astype(jnp.int32)
 
 
-def pack_kernel(links_ref, k_ref, v_ref, q_ref, g_ref, kv_ref, qg_ref, most_ref, held, sems):
+def pack_kernel(
+    links_ref, k_ref, v_ref, q_ref, g_ref, kv_ref, qg_ref, most_ref, held, links, sems, links_sem
+):
     copies = [
         pltpu.make_async_copy(ref, held.at[i], sems.at[i])
         for i, ref in enumerate((k_ref, v_ref, q_ref, g_ref))
     ]
-    for copy in copies:
+    links_copy = pltpu.make_async_copy(links_ref, links, links_sem)
+    for copy in (*copies, links_copy):
         copy.start()
-    most_ref[0] = most_far(links_ref, kv_ref.shape[0])
     for first, out_ref in ((0, kv_ref), (2, qg_ref)):
         copies[first].wait()
         copies[first + 1].wait()
         for h in range(out_ref.shape[0]):
             cols = slice(h * HD, (h + 1) * HD)
             out_ref[h] = jnp.concatenate([held[first, :, cols], held[first + 1, :, cols]], axis=1)
+    links_copy.wait()
+    most_ref[0] = most_far(links, kv_ref.shape[0])
 
 
 def own_tiles(all_ref, index, held, sems):
@@ -285,11 +289,13 @@
             jax.ShapeDtypeStruct((blocks, BLK, PAIR), bf),
             jax.ShapeDtypeStruct((1,), jnp.int32),
         ),
-        in_specs=[VMEM] + [ANY] * 4,
+        in_specs=[ANY] * 5,
         out_specs=(VMEM, VMEM, SMEM),
         scratch_shapes=[
             pltpu.VMEM((4, *queries.shape), bf),
+            pltpu.VMEM((links.shape[1], links.shape[2], links.shape[0]), jnp.int32),
             pltpu.SemaphoreType.DMA((4,)),
+            pltpu.SemaphoreType.DMA,
         ],
         cost_estimate=cost(0, 16 * blocks * BLK * PAIR),
         name="pack",

time: 199 us -> 198 us (level)
  no operation moved by 1% of the time
where the time goes in v7:
time: 198 us; the launch traced here: 197 us
  waiting for transfers between devices  63.2 us (32%)
  blocking collectives  48.1 us (24%)
  starting transfers between devices  45.3 us (23%)
  Pallas kernels  17.6 us (9%)
  between operations  14.7 us (7%)
  other arithmetic  4.01 us (2%)
  local copies, waits for them, and re-layouts  3.6 us (2%)
    all_to_all x1, blocking collectives, step(): dkv = lax.all_to_all(dkv, 'head', split_axis=0, concat_axis=0, tiled=True)  24.7 us
    all_to_all x1, blocking collectives, step(): lax.all_to_all(summed, 'slab', split_axis=0, concat_axis=0, tiled=True)  23.4 us
    all_to_all x1, starting transfers between devices, step(): near = lax.all_to_all(kv, 'head', split_axis=0, concat_axis=0, tiled=True)  18.2 us
    all_to_all x1, waiting for transfers between devices, step(): lax.all_to_all(chosen, 'slab', split_axis=0, concat_axis=0, tiled=True)  17.2 us
    all_to_all x1, waiting for transfers between devices, step(): near = lax.all_to_all(kv, 'head', split_axis=0, concat_axis=0, tiled=True)  15.2 us
    all_to_all x1, waiting for transfers between devices, step(): lax.all_to_all(far_out, 'slab', split_axis=0, concat_axis=0, tiled=True)  15.2 us
    all_to_all x1, waiting for transfers between devices, step(): lax.all_to_all(pieces, 'slab', split_axis=0, concat_axis=0, tiled=True)  14.9 us
    all_to_all x1, starting transfers between devices, step(): lax.all_to_all(pieces, 'slab', split_axis=0, concat_axis=0, tiled=True)  13.2 us
  transfers between devices with their start and end apart: 6, of which 4 were waited for; matrix products, arithmetic and copies ran while one was open for 3% of the time, Pallas kernels for 2%

profile of v7, /device:TPU:1, one launch (start us, length us, event | category | flops | bytes accessed | tf_op | source)
XLA Modules:
  0.0 197.3 jit_solution(3047699745814959730)
XLA Ops:
  7.2 2.5 %pack.1 = (bf16[16,128,128]{2,1,0:T(8,128)(2,1)}, bf16[16,128,128]{2,1,0:T(8,128)(2,1)}, s32[1]{0:T(128)}) custom-call(s32[40,2,64]{2,1,0:T(2,128)} %bitcast.62, bf16[128,1024]{1,0:T(8,128)(2,1)} %k_ref.1, bf16[128,1024]{1,0:T(8,128)(2,1)} %v_ref.1, bf16[128,1024]{1,0:T(8,128)(2,1)} %q_ref.1, bf16[128,1024]{1,0:T(8,128)(2,1)} %g_ref.1), custom_call_target="tpu_custom_call" | custom-call | bytes 4194304 | tf_op jit(solution)/shard_map/pack/pallas_call | solution.py:285
  10.3 180.2 %conditional.1 = ((bf16[128,1024]{1,0:T(8,128)(2,1)}, bf16[128,1024]{1,0:T(8,128)(2,1)}, bf16[128,1024]{1,0:T(8,128)(2,1)}, bf16[128,1024]{1,0:T(8,128)(2,1)})) conditional(s32[]{:T(128)} %bitcast.33, (bf16[16,128,128]{2,1,0:T(8,128)(2,1)}, s32[64,40,2]{0,2,1:T(2,128)}, s32[64,64]{1,0:T(8,128)}, bf16[16,128,128]{2,1,0:T(8,128)(2,1)}) %tuple.17, ...), branch_computations={%region_0.4_spmd, %region_4.8_spmd} | conditional | flops 2624773120 | bytes 97220160 | solution.py:306
  11.3 18.2 %all-to-all-start.6 = ((bf16[16,128,128]{2,1,0:T(8,128)(2,1)}), bf16[16,128,128]{2,1,0:T(8,128)(2,1)S(1)}, u32[]{:S(2)}, u32[]{:S(2)}) async-start(bf16[16,128,128]{2,1,0:T(8,128)(2,1)} %get-tuple-element.27), calls=%async_computation.6 | async-start | bytes 1048576 | tf_op jit(solution)/shard_map/cond/branch_1_fun/all_to_all | solution.py:349
  29.5 0.8 copy.55
  31.6 15.2 %all-to-all-done.6.near_ref = bf16[16,128,128]{2,1,0:T(8,128)(2,1)S(1)} async-done(((bf16[16,128,128]{2,1,0:T(8,128)(2,1)}), bf16[16,128,128]{2,1,0:T(8,128)(2,1)S(1)}, u32[]{:S(2)}, u32[]{:S(2)}) %all-to-all-start.6) | async-done | bytes 524320 | tf_op jit(solution)/shard_map/cond/branch_1_fun/all_to_all | solution.py:349
  46.8 1.9 spread.3
  48.7 13.2 %all-to-all-start.7 = ((bf16[64,32,128]{2,1,0:T(8,128)(2,1)}), bf16[64,32,128]{2,1,0:T(8,128)(2,1)S(1)}, u32[]{:S(2)}, u32[]{:S(2)}) async-start(bf16[64,32,128]{2,1,0:T(8,128)(2,1)} %bitcast.17), calls=%async_computation.7 | async-start | bytes 1048576 | tf_op jit(solution)/shard_map/cond/branch_1_fun/all_to_all | solution.py:362
  62.7 0.8 add_add_fusion.1
  63.4 1.2 select_reduce_fusion.2
  65.1 14.9 %all-to-all-done.7 = bf16[64,32,128]{2,1,0:T(8,128)(2,1)S(1)} async-done(((bf16[64,32,128]{2,1,0:T(8,128)(2,1)}), bf16[64,32,128]{2,1,0:T(8,128)(2,1)S(1)}, u32[]{:S(2)}, u32[]{:S(2)}) %all-to-all-start.7) | async-done | bytes 524320 | tf_op jit(solution)/shard_map/cond/branch_1_fun/all_to_all | solution.py:362
  80.0 0.7 gather.3
  80.8 0.8 copy-done.3
  81.6 6.3 %all-to-all-start.8 = ((bf16[64,32,128]{2,1,0:T(8,128)(2,1)}), bf16[64,32,128]{2,1,0:T(8,128)(2,1)S(1)}, u32[]{:S(2)}, u32[]{:S(2)}) async-start(bf16[64,32,128]{2,1,0:T(8,128)(2,1)} %bitcast.49), calls=%async_computation.8 | async-start | bytes 1048576 | tf_op jit(solution)/shard_map/cond/branch_1_fun/all_to_all | solution.py:374
  88.0 17.2 %all-to-all-done.8 = bf16[64,32,128]{2,1,0:T(8,128)(2,1)S(1)} async-done(((bf16[64,32,128]{2,1,0:T(8,128)(2,1)}), bf16[64,32,128]{2,1,0:T(8,128)(2,1)S(1)}, u32[]{:S(2)}, u32[]{:S(2)}) %all-to-all-start.8) | async-done | bytes 524320 | tf_op jit(solution)/shard_map/cond/branch_1_fun/all_to_all | solution.py:374
  105.2 0.8 copy-done.7
  106.0 8.2 %attend.3 = (bf16[16,128,128]{2,1,0:T(8,128)(2,1)}, f32[16,128,128]{2,1,0:T(8,128)}, bf16[2048,128]{1,0:T(8,128)(2,1)}) custom-call(s32[1]{0:T(128)} %bitcast.16.index_ref, s32[80]{0:T(128)} %reshape.103.links_ref, bf16[16,128,128]{2,1,0:T(8,128)(2,1)} %copy-done.1, bf16[2048,128]{1,0:T(8,128)(2,1)} %bitcast.59, bf16[16,16,128,128]{3,2,1,0:T(8,128)(2,1)} %bitcast.55), custom_call_target="tpu_custom_call" | custom-call | flops 1006632960 | bytes 3145728 | tf_op jit(solution)/shard_map/cond/branch_1_fun/attend/pallas_call | solution.py:376
  114.2 7.4 %all-to-all-start.9 = ((bf16[64,32,128]{2,1,0:T(8,128)(2,1)}), bf16[64,32,128]{2,1,0:T(8,128)(2,1)S(1)}, u32[]{:S(2)}, u32[]{:S(2)}) async-start(bf16[64,32,128]{2,1,0:T(8,128)(2,1)} %bitcast.61), calls=%async_computation.9 | async-start | bytes 1048576 | tf_op jit(solution)/shard_map/cond/branch_1_fun/all_to_all | solution.py:412
  121.7 0.9 fusion.8.hot_ref
  122.6 15.2 %all-to-all-done.9 = bf16[64,32,128]{2,1,0:T(8,128)(2,1)S(1)} async-done(((bf16[64,32,128]{2,1,0:T(8,128)(2,1)}), bf16[64,32,128]{2,1,0:T(8,128)(2,1)S(1)}, u32[]{:S(2)}, u32[]{:S(2)}) %all-to-all-start.9) | async-done | bytes 524320 | tf_op jit(solution)/shard_map/cond/branch_1_fun/all_to_all | solution.py:412
  137.7 0.7 reduce.7
  138.4 23.4 %all_to_all.84 = bf16[64,32,128]{2,1,0:T(8,128)(2,1)S(1)} all-to-all(bf16[64,32,128]{2,1,0:T(8,128)(2,1)S(1)} %bitcast.53), channel_id=1, replica_groups=mesh['slab'=64,'head'=16] {'slab'}, dimensions={0} | all-to-all | bytes 1048576 | tf_op jit(solution)/shard_map/cond/branch_1_fun/all_to_all | solution.py:426
  161.9 0.8 combine.3
  162.7 24.7 %all_to_all.85.dkv_ref = bf16[16,128,128]{2,1,0:T(8,128)(2,1)} all-to-all(bf16[16,128,128]{2,1,0:T(8,128)(2,1)S(1)} %combine.3), channel_id=1, replica_groups=mesh['slab'=64,'head'=16] {'head'}, dimensions={0} | all-to-all | bytes 1048576 | tf_op jit(solution)/shard_map/cond/branch_1_fun/all_to_all | solution.py:441
  187.4 2.8 %unpack.3 = (bf16[128,1024]{1,0:T(8,128)(2,1)}, bf16[128,1024]{1,0:T(8,128)(2,1)}, bf16[128,1024]{1,0:T(8,128)(2,1)}, bf16[128,1024]{1,0:T(8,128)(2,1)}) custom-call(s32[1]{0:T(128)} %bitcast.16.index_ref, bf16[16,16,128,128]{3,2,1,0:T(8,128)(2,1)} %bitcast.57, bf16[16,128,128]{2,1,0:T(8,128)(2,1)} %all_to_all.85.dkv_ref), custom_call_target="tpu_custom_call" | custom-call | bytes 2097152 | tf_op jit(solution)/shard_map/cond/branch_1_fun/unpack/pallas_call | solution.py:442
  (30 shorter events, 3.3 us)
Async XLA Ops:
  10.5 94.7 %all-gather.13.cloned.1.call-start = ((), (), s32[]{:S(2)}) async-start(), calls=%async_computation.14 | async-start | bytes 8912896 | tf_op jit(solution)/shard_map/cond/branch_1_fun/all_gather | solution.py:350
  11.3 35.5 %all-to-all-start.6 = ((bf16[16,128,128]{2,1,0:T(8,128)(2,1)}), bf16[16,128,128]{2,1,0:T(8,128)(2,1)S(1)}, u32[]{:S(2)}, u32[]{:S(2)}) async-start(bf16[16,128,128]{2,1,0:T(8,128)(2,1)} %get-tuple-element.27), calls=%async_computation.6 | async-start | bytes 1048576 | tf_op jit(solution)/shard_map/cond/branch_1_fun/all_to_all | solution.py:349
  46.8 34.8 %copy-start.1 = (bf16[16,128,128]{2,1,0:T(8,128)(2,1)}, bf16[16,128,128]{2,1,0:T(8,128)(2,1)S(1)}, u32[]{:S(2)}) copy-start(bf16[16,128,128]{2,1,0:T(8,128)(2,1)S(1)} %all-to-all-done.6.near_ref) | copy-start | bytes 1572868 | tf_op jit(solution)/shard_map/cond
  48.7 31.3 %all-to-all-start.7 = ((bf16[64,32,128]{2,1,0:T(8,128)(2,1)}), bf16[64,32,128]{2,1,0:T(8,128)(2,1)S(1)}, u32[]{:S(2)}, u32[]{:S(2)}) async-start(bf16[64,32,128]{2,1,0:T(8,128)(2,1)} %bitcast.17), calls=%async_computation.7 | async-start | bytes 1048576 | tf_op jit(solution)/shard_map/cond/branch_1_fun/all_to_all | solution.py:362
  80.7 0.8 copy-start.3
  81.6 23.6 %all-to-all-start.8 = ((bf16[64,32,128]{2,1,0:T(8,128)(2,1)}), bf16[64,32,128]{2,1,0:T(8,128)(2,1)S(1)}, u32[]{:S(2)}, u32[]{:S(2)}) async-start(bf16[64,32,128]{2,1,0:T(8,128)(2,1)} %bitcast.49), calls=%async_computation.8 | async-start | bytes 1048576 | tf_op jit(solution)/shard_map/cond/branch_1_fun/all_to_all | solution.py:374
  87.9 99.5 %all-gather.15.cloned.1.call-start = ((), (), s32[]{:S(2)}) async-start(), calls=%async_computation.15 | async-start | bytes 8912896 | tf_op jit(solution)/shard_map/cond/branch_1_fun/all_gather | solution.py:408
  105.2 0.8 copy-start.7
  114.2 23.5 %all-to-all-start.9 = ((bf16[64,32,128]{2,1,0:T(8,128)(2,1)}), bf16[64,32,128]{2,1,0:T(8,128)(2,1)S(1)}, u32[]{:S(2)}, u32[]{:S(2)}) async-start(bf16[64,32,128]{2,1,0:T(8,128)(2,1)} %bitcast.61), calls=%async_computation.9 | async-start | bytes 1048576 | tf_op jit(solution)/shard_map/cond/branch_1_fun/all_to_all | solution.py:412
  137.7 24.2 %copy-start.5 = (f32[16,128,128]{2,1,0:T(8,128)S(1)}, f32[16,128,128]{2,1,0:T(8,128)}, u32[]{:S(2)}) copy-start(f32[16,128,128]{2,1,0:T(8,128)} %get-tuple-element.34.home_ref) | copy-start | bytes 3145732 | tf_op jit(solution)/shard_map/cond
Sparse Core Ops, SparseCore 0:
  14.1 75.7 all-gather.12
  114.3 54.9 all-gather.14
